TPU v7x, 32 devices: a whole 2x2x4 slice. The times are simulated.
32 devices in a mesh: gx: 4 (over z), gy: 4 (over y, x), gz: 2 (over core).
Axes of the slice: x: 2, y: 2, z: 4, core: 2. Of those that a mesh axis runs over, the one named last changes fastest.
Arguments:
- fine_state: float32 [64, 5, 32, 1024], P(('gx', 'gy', 'gz')), may hold values from -1.2 to 3.5, as said below
- coarse_state: float32 [128, 5, 16, 256], P(('gx', 'gy', 'gz')), may hold values from -1.2 to 3.5, as said below
- neighbours: int32 [64, 6], P(('gx', 'gy', 'gz')), may hold values from -1 to 63, as said below
- coarse_sources: int32 [64, 6], P(('gx', 'gy', 'gz')), may hold values from -1 to 127, as said below
- covering: int32 [128], P(('gx', 'gy', 'gz')), may hold values from -1 to 63, as said below
Outputs:
- fine_next: float32 [64, 5, 32, 1024], P(('gx', 'gy', 'gz'))
- coarse_next: float32 [128, 5, 16, 256], P(('gx', 'gy', 'gz'))
Inputs may be any that keep to these rules, and one draw needn't show every extreme that they name: `fine_state`: each cell is the conserved state of density 0.5 to 2, velocity components -0.6 to 0.6 and pressure 0.4 to 1.6. `coarse_state`: each cell is the conserved state of density 0.5 to 2, velocity components -0.6 to 0.6 and pressure 0.4 to 1.6. For each box face exactly one of neighbours and coarse_sources is not -1; every box or block named lies on a device with the same gx index as the box; the faces of one device's boxes name at most 2 boxes or blocks held by any one device, and exactly 2 on some device. `coarse_sources`: see neighbours. `covering`: every fine box is named by exactly one block; a block and the box it names lie on devices with the same gy and gz index; the blocks of one device name at most 1 boxes of any one device, and exactly 1 of some device.
All inputs are finite; a program needn't handle non-finite values.
Results may differ from a plain program's by a relative error of at most 0.00005.
Values sent between devices are 32-bit elements; how exact they have to be, the bound alone decides.
A program may use at most 64 MiB of HBM per device.

v0:
```python
import jax
import jax.numpy as jnp
from jax import lax
from jax.sharding import PartitionSpec as P

adiabatic = 5.0 / 3.0
courant = 0.12
highest = lax.Precision.HIGHEST


def edge_flux(left_state, right_state, normal):
    fluxes = []
    speeds = []
    for current in (left_state, right_state):
        density = current[:, 0]
        normal_speed = current[:, normal] / density
        kinetic = (
            0.5
            * (
                current[:, 1] * current[:, 1]
                + current[:, 2] * current[:, 2]
                + current[:, 3] * current[:, 3]
            )
            / density
        )
        pressure = (adiabatic - 1.0) * (current[:, 4] - kinetic)
        sound_speed = jnp.sqrt(adiabatic * pressure / density)
        entries = [
            current[:, normal],
            current[:, 1] * normal_speed,
            current[:, 2] * normal_speed,
            current[:, 3] * normal_speed,
            (current[:, 4] + pressure) * normal_speed,
        ]
        entries[normal] = entries[normal] + pressure
        fluxes.append(jnp.stack(entries, axis=1))
        speeds.append(jnp.abs(normal_speed) + sound_speed)
    fastest = jnp.maximum(speeds[0], speeds[1])
    return 0.5 * (fluxes[0] + fluxes[1]) - 0.5 * fastest[:, None] * (right_state - left_state)


def lateral_picks(edge_cells):
    plane_cells = edge_cells * edge_cells
    place = jnp.arange(plane_cells, dtype=jnp.int32)[:, None]
    inner = jnp.arange(edge_cells, dtype=jnp.int32)[None, :]
    tables = [
        place == inner,
        place == (edge_cells - 1) * edge_cells + inner,
        place == inner * edge_cells,
        place == inner * edge_cells + edge_cells - 1,
    ]
    return [table.astype(jnp.float32) for table in tables]


def face_tables(states, edge_cells):
    plane_cells = edge_cells * edge_cells
    item_count = states.shape[0]
    picks = jnp.concatenate(lateral_picks(edge_cells), axis=1)
    lateral = jnp.dot(
        states.reshape(item_count * 5 * edge_cells, plane_cells),
        picks,
        precision=highest,
        preferred_element_type=jnp.float32,
    )
    lateral = (
        lateral.reshape(item_count, 5, edge_cells, 4, edge_cells)
        .transpose(0, 3, 1, 2, 4)
        .reshape(item_count, 4, 5, plane_cells)
    )
    outer = jnp.stack([states[:, :, 0, :], states[:, :, edge_cells - 1, :]], axis=1)
    return jnp.concatenate([outer, lateral], axis=1).reshape(item_count * 6 * 5, plane_cells)


def lookup(requests, face_table):
    flat_codes = requests.reshape(-1)
    codes = 1 + jnp.arange(face_table.shape[0], dtype=jnp.int32)
    picks = (flat_codes[:, None] == codes[None, :]).astype(jnp.float32)
    answers = jnp.dot(picks, face_table, precision=highest, preferred_element_type=jnp.float32)
    return answers.reshape(requests.shape + (face_table.shape[1],))


def body(fine_state, coarse_state, neighbours, coarse_sources, covering):
    box_count = fine_state.shape[0]
    components = fine_state.shape[1]
    edge_cells = fine_state.shape[2]
    plane_cells = fine_state.shape[3]
    blocks = coarse_state.shape[0]
    half_cells = coarse_state.shape[2]
    small_plane = coarse_state.shape[3]
    line_size = lax.axis_size("gy") * lax.axis_size("gz")
    face_count = box_count * 6
    slot_count = -(-face_count // line_size)
    side_index = jnp.arange(6, dtype=jnp.int32)
    facing = jnp.broadcast_to(jnp.bitwise_xor(side_index, 1), (box_count, 6)).reshape(-1)
    fine_ids = neighbours.reshape(-1)
    coarse_ids = coarse_sources.reshape(-1)
    is_fine = fine_ids >= 0
    source_dev = jnp.where(is_fine, fine_ids // box_count, coarse_ids // blocks)
    peer_index = source_dev % line_size
    request_code = jnp.where(
        is_fine,
        1 + fine_ids % box_count * 6 + facing,
        1 + face_count + coarse_ids % blocks * 6 + facing,
    )
    to_peer = (peer_index[:, None] == jnp.arange(line_size, dtype=jnp.int32)[None, :]).astype(
        jnp.int32
    )
    peer_rank = jnp.sum((jnp.cumsum(to_peer, axis=0) - to_peer) * to_peer, axis=1)
    at_rank = (peer_rank[:, None] == jnp.arange(slot_count, dtype=jnp.int32)[None, :]).astype(
        jnp.int32
    )
    requests = jnp.sum(
        to_peer[:, :, None] * at_rank[:, None, :] * request_code[:, None, None], axis=0
    )
    fine_faces = face_tables(fine_state, edge_cells).reshape(face_count, components * plane_cells)
    fine_place = jnp.arange(plane_cells, dtype=jnp.int32)
    coarse_of_fine = fine_place // edge_cells // 2 * half_cells + fine_place % edge_cells // 2
    widen = (jnp.arange(small_plane, dtype=jnp.int32)[:, None] == coarse_of_fine[None, :]).astype(
        jnp.float32
    )
    coarse_faces = jnp.dot(
        face_tables(coarse_state, half_cells),
        widen,
        precision=highest,
        preferred_element_type=jnp.float32,
    )
    coarse_faces = coarse_faces.reshape(blocks * 6, components * plane_cells)
    face_table = jnp.concatenate([fine_faces, coarse_faces], axis=0)
    replies = lax.all_to_all(
        lookup(
            lax.all_to_all(requests, ("gy", "gz"), split_axis=0, concat_axis=0, tiled=True),
            face_table,
        ),
        ("gy", "gz"),
        split_axis=0,
        concat_axis=0,
        tiled=True,
    )
    replies = replies.reshape(line_size * slot_count, components * plane_cells)
    chosen = (
        (peer_index * slot_count + peer_rank)[:, None]
        == jnp.arange(line_size * slot_count, dtype=jnp.int32)[None, :]
    ).astype(jnp.float32)
    ghosts = jnp.dot(
        chosen, replies, precision=highest, preferred_element_type=jnp.float32
    ).reshape(box_count, 6, components, plane_cells)
    spread_tables = [jnp.transpose(table) for table in lateral_picks(edge_cells)]
    full_shape = (box_count, components, edge_cells, plane_cells)

    def spread(layer, table):
        flat_layer = layer.reshape(box_count * components * edge_cells, edge_cells)
        return jnp.dot(
            flat_layer, table, precision=highest, preferred_element_type=jnp.float32
        ).reshape(full_shape)

    inner_x = edge_flux(fine_state[:, :, :-1], fine_state[:, :, 1:], 1)
    low_x = edge_flux(ghosts[:, 0], fine_state[:, :, 0], 1)
    high_x = edge_flux(fine_state[:, :, edge_cells - 1], ghosts[:, 1], 1)
    step_x = jnp.concatenate([inner_x, high_x[:, :, None]], axis=2) - jnp.concatenate(
        [low_x[:, :, None], inner_x], axis=2
    )
    row_of = fine_place // edge_cells
    col_of = fine_place % edge_cells
    above_y = jnp.where(
        row_of == edge_cells - 1,
        spread(ghosts[:, 3], spread_tables[1]),
        jnp.roll(fine_state, -edge_cells, axis=3),
    )
    below_y = jnp.where(
        row_of == 0,
        spread(ghosts[:, 2], spread_tables[0]),
        jnp.roll(fine_state, edge_cells, axis=3),
    )
    step_y = edge_flux(fine_state, above_y, 2) - edge_flux(below_y, fine_state, 2)
    above_z = jnp.where(
        col_of == edge_cells - 1,
        spread(ghosts[:, 5], spread_tables[3]),
        jnp.roll(fine_state, -1, axis=3),
    )
    below_z = jnp.where(
        col_of == 0, spread(ghosts[:, 4], spread_tables[2]), jnp.roll(fine_state, 1, axis=3)
    )
    step_z = edge_flux(fine_state, above_z, 3) - edge_flux(below_z, fine_state, 3)
    updated = fine_state - courant * (step_x + step_y + step_z)
    shrink = jnp.transpose(widen)
    reduced = jnp.dot(
        updated.reshape(box_count * components * edge_cells, plane_cells),
        shrink,
        precision=highest,
        preferred_element_type=jnp.float32,
    )
    reduced = reduced.reshape(box_count, components, half_cells, 2, small_plane)
    restricted = 0.125 * (reduced[:, :, :, 0] + reduced[:, :, :, 1])
    block_rows = restricted.reshape(box_count, components * half_cells * small_plane)
    covered = covering >= 0
    owner_device = covering // box_count
    column = owner_device // line_size
    gathered_index = column * box_count + covering % box_count
    portion = lax.all_gather(block_rows, "gx", axis=0, tiled=True)
    row_count = portion.shape[0]
    matches = (
        gathered_index[:, None] == jnp.arange(row_count, dtype=jnp.int32)[None, :]
    ) & covered[:, None]
    placed = jnp.dot(
        matches.astype(jnp.float32), portion, precision=highest, preferred_element_type=jnp.float32
    )
    coarse_next = jnp.where(
        covered[:, None, None, None], placed.reshape(coarse_state.shape), coarse_state
    )
    return (updated, coarse_next)


def solution(mesh):
    in_specs = (
        P(("gx", "gy", "gz"), None, None, None),
        P(("gx", "gy", "gz"), None, None, None),
        P(("gx", "gy", "gz"), None),
        P(("gx", "gy", "gz"), None),
        P(("gx", "gy", "gz")),
    )
    out_specs = (P(("gx", "gy", "gz"), None, None, None), P(("gx", "gy", "gz"), None, None, None))
    return jax.shard_map(body, mesh=mesh, in_specs=in_specs, out_specs=out_specs, check_vma=False)
```

profile of v0, /device:TPU:0, one launch (start us, length us, event | category | flops | bytes accessed | tf_op | source)
XLA Modules:
  0.0 116.8 jit_solution(2005562917430846387)
XLA Ops:
  0.7 0.8 reshape.654
  1.5 0.8 reshape.655
  3.3 5.2 %all-to-all-start = ((s32[8,1,2]{2,1,0:T(1,128)}), s32[8,1,2]{2,1,0:T(1,128)}, u32[]{:S(2)}, u32[]{:S(2)}) async-start(s32[8,1,2]{2,1,0:T(1,128)} %copy.102), calls=%async_computation | async-start | bytes 8192 | tf_op jit(solution)/shard_map/all_to_all | solution.py:131
  10.9 1.8 %fusion.87 = (f32[2,5,1,1024]{3,2,1,0:T(1,128)}, f32[2,1,5,1024]{3,1,2,0:T(1,128)S(1)}, f32[2,5,1,1024]{3,2,1,0:T(1,128)}) fusion(f32[2,5,32,1024]{3,2,1,0:T(8,128)} %param.5), kind=kLoop, calls=%fused_computation.287 | loop fusion | bytes 204800 | tf_op jit(solution)/shard_map/slice | solution.py:158
  12.7 4.0 %fusion.84 = (f32[2,5,32,992]{3,2,1,0:T(8,128)}, f32[2,5,32,992]{3,2,1,0:T(8,128)}) fusion(f32[2,5,32,1024]{3,2,1,0:T(8,128)} %param.5), kind=kLoop, calls=%fused_computation.284 | loop fusion | bytes 5079040 | tf_op jit(solution)/shard_map/jit(_roll_static)/slice | solution.py:172
  16.6 0.8 fusion.83
  18.0 0.8 fusion.86
  20.5 1.3 %multiply_bitcast_fusion.4 = (f32[2,31,1024]{2,1,0:T(8,128)}, f32[2,1,31,1024]{3,2,1,0:T(8,128)}, f32[2,1,31,1024]{3,2,1,0:T(8,128)S(1)}, f32[2,1,31,1024]{3,2,1...) fusion(f32[2,5,32,1024]{3,2,1,0:T(8,128)S(1)} %copy-done), kind=kLoop, calls=%fused_computation.71 | loop fusion | flops 1777663 | bytes 4087808 | tf_op jit(solution)/shard_map/mul | solution.py:39
  23.2 0.8 convolution_bitcast_fusion
  24.7 0.8 copy.211
  25.9 0.9 copy.146
  28.9 0.8 pad_maximum_fusion.1
  31.6 0.8 add_dynamic-update-slice_fusion.6
  32.4 0.7 multiply_dynamic-update-slice_fusion.20
  33.1 0.7 multiply_dynamic-update-slice_fusion.19
  33.8 0.8 multiply_dynamic-update-slice_fusion.18
  36.1 1.6 %multiply_subtract_fusion = f32[2,5,31,1024]{3,2,1,0:T(8,128)} fusion(f32[2,5,32,1024]{3,2,1,0:T(8,128)S(1)} %copy-done, f32[2,5,31,1024]{3,2,1,0:T(8,128)S(1)} %multiply_dynamic-update-slice_fusion.21, f32[2,5,31,1024]{3,2,1,0:T(8,128)S(1)} %copy-done.9, f32[2,31,1024]{2,1,0:T(8,128)S(1)} %copy-done.18), kind=kLoop, calls=%fused_computation.11 | loop fusion | flops 1587200 | bytes 6602752 | tf_op jit(solution)/shard_map/sub | solution.py:39
  38.4 1.3 %reduce.11 = s32[8,2]{1,0:T(8,128)S(1)} reduce(s32[8,1,2]{2,1,0:T(1,128)} %all-to-all-done, s32[]{:T(128)} %broadcast.765), dimensions={1}, to_apply=%all_to_all.10.reduce_sub_computation.3 | reduce | bytes 132 | tf_op jit(solution)/shard_map/all_to_all | solution.py:131
  40.3 0.9 reshape.665
  41.2 4.2 %all-to-all-start.1 = ((f32[8,2,5120]{2,1,0:T(2,128)}), f32[8,2,5120]{2,1,0:T(2,128)S(1)}, u32[]{:S(2)}, u32[]{:S(2)}) async-start(f32[8,2,5120]{2,1,0:T(2,128)} %reshape.665), calls=%async_computation.1 | async-start | bytes 655360 | tf_op jit(solution)/shard_map/all_to_all | solution.py:129
  45.4 2.0 %fusion.85 = (f32[2,5,32,1023]{3,2,1,0:T(8,128)}, f32[2,5,32,1023]{3,2,1,0:T(8,128)}) fusion(f32[2,5,32,1024]{3,2,1,0:T(8,128)S(1)} %copy-done), kind=kLoop, calls=%fused_computation.285 | loop fusion | bytes 5237760 | tf_op jit(solution)/shard_map/jit(_roll_static)/slice | solution.py:178
  47.4 5.7 %all-to-all-done.1 = f32[8,2,5120]{2,1,0:T(2,128)S(1)} async-done(((f32[8,2,5120]{2,1,0:T(2,128)}), f32[8,2,5120]{2,1,0:T(2,128)S(1)}, u32[]{:S(2)}, u32[]{:S(2)}) %all-to-all-start.1) | async-done | bytes 327712 | tf_op jit(solution)/shard_map/all_to_all | solution.py:129
  54.4 1.6 %slice_reduce_fusion.3 = (f32[2,5,1024]{2,1,0:T(8,128)S(1)}, f32[2,5,1024]{2,1,0:T(8,128)}, f32[2,5,1024]{2,1,0:T(8,128)}, f32[2,5,1024]{2,1,0:T(8,128)}, f32[2,...) fusion(f32[2,6,5,1024]{3,1,2,0:T(8,128)S(1)} %fusion.22), kind=kLoop, calls=%fused_computation.127 | loop fusion | bytes 491520 | tf_op jit(solution)/shard_map/slice | solution.py:166
  56.1 2.0 %convolution_select_fusion.3 = f32[2,5,32,1024]{3,2,1,0:T(8,128)S(1)} fusion(f32[2,5,32,32]{3,2,1,0:T(8,128)S(1)} %dot_general.60, f32[2,5,32,32]{3,2,1,0:T(8,128)S(1)} %copy-done.23, f32[2,5,32,992]{3,2,1,0:T(8,128)} %get-tuple-element.50, pred[1024]{0:T(1024)(128)(4,1)S(1)} %copy-done.49, s32[32]{0:T(128)S(1)} %copy-done.45), kind=kOutput, calls=%fused_computation.3 | convolution fusion | flops 126517248 | bytes 2663552 | tf_op jit(solution)/shard_map/dot_general | solution.py:152
  58.1 1.4 %multiply_bitcast_fusion.3 = (f32[2,32,1024]{2,1,0:T(8,128)}, f32[2,1,32,1024]{3,2,1,0:T(8,128)}, f32[2,1,32,1024]{3,2,1,0:T(8,128)S(1)}, f32[2,1,32,1024]{3,2,1...) fusion(f32[2,5,32,1024]{3,2,1,0:T(8,128)S(1)} %convolution_sele, ...), kind=kLoop, calls=%fused_computation.58 | loop fusion | flops 1835005 | bytes 4980736 | tf_op jit(solution)/shard_map/mul | solution.py:39
  59.7 1.0 copy-done.13
  60.8 1.6 %dot_general.64 = f32[2,5,32,32]{3,2,1,0:T(8,128)} reshape(f32[2,5,1024]{2,1,0:T(8,128)} %get-tuple-element.4) | data formatting | bytes 81920 | tf_op jit(solution)/shard_map/dot_general | solution.py:152
  62.4 1.6 %dot_general.62 = f32[2,5,32,32]{3,2,1,0:T(8,128)} reshape(f32[2,5,1024]{2,1,0:T(8,128)} %get-tuple-element.5) | data formatting | bytes 81920 | tf_op jit(solution)/shard_map/dot_general | solution.py:152
  64.8 0.8 add_dynamic-update-slice_fusion.5
  65.6 0.8 convolution_select_fusion.1
  67.9 1.5 %multiply_bitcast_fusion.2 = (f32[2,32,1024]{2,1,0:T(8,128)}, f32[2,1,32,1024]{3,2,1,0:T(8,128)S(1)}, f32[2,1,32,1024]{3,2,1,0:T(8,128)S(1)}, f32[2,5,32,1024]{3...) fusion(f32[2,5,32,1024]{3,2,1,0:T(8,128)S(1)} %convolution_sele, ...), kind=kLoop, calls=%fused_computation.52 | loop fusion | flops 2359294 | bytes 6291456 | tf_op jit(solution)/shard_map/mul | solution.py:39
  69.7 1.0 copy-done.12
  70.7 1.1 copy-done.10
  71.8 0.7 multiply_dynamic-update-slice_fusion.8
  72.6 0.7 multiply_dynamic-update-slice_fusion.7
  73.3 1.6 %dot_general.66 = f32[2,5,32,32]{3,2,1,0:T(8,128)} reshape(f32[2,5,1024]{2,1,0:T(8,128)} %get-tuple-element.3) | data formatting | bytes 81920 | tf_op jit(solution)/shard_map/dot_general | solution.py:152
  74.9 2.2 %convolution_select_fusion = f32[2,5,32,1024]{3,2,1,0:T(8,128)S(1)} fusion(f32[2,5,32,32]{3,2,1,0:T(8,128)} %dot_general.66, f32[2,5,32,1023]{3,2,1,0:T(8,128)} %get-tuple-element.53, f32[2,5,32,1]{3,2,1,0:T(8,128)} %get-tuple-element.55, pred[1024]{0:T(1024)(128)(4,1)S(1)} %copy-done.46, s32[32]{0:T(128)S(1)} %copy-done.41), kind=kOutput, calls=%fused_computation | convolution fusion | flops 126517248 | bytes 2663552 | tf_op jit(solution)/shard_map/dot_general | solution.py:152
  77.2 1.3 %multiply_dynamic-update-slice_fusion.15 = (f32[2,5,32,1024]{3,2,1,0:T(8,128)}, f32[2,5,32,1024]{3,2,1,0:T(8,128)}, f32[2,5,32,1024]{3,2,1,0:T(8,128)S(1)}, f32[...) fusion(f32[2,5,32,1024]{3,2,1,0:T(8,128)} %get-tuple-element.63, ...), kind=kLoop, calls=%fused_computation.66 | loop fusion | flops 1441791 | bytes 4456448 | tf_op jit(solution)/shard_map/stack | solution.py:36
  78.5 0.7 multiply_dynamic-update-slice_fusion.6
  79.5 1.1 copy-done.11
  83.1 0.8 stack.153
  84.6 0.8 stack.141
  85.4 1.3 %fusion.30 = (f32[2,5,1,1024]{3,2,1,0:T(1,128)S(1)}, f32[2,5,1,1024]{3,2,1,0:T(1,128)S(1)}) fusion(f32[2,5,1,1024]{3,1,2,0:T(8,128)} %add.576, f32[2,1024]{1,0:T(2,128)S(1)} %bitcast.193, f32[2,6,5,1024]{3,1,2,0:T(8,128)} %copy-done.16, f32[2,5,32,1024]{3,2,1,0:T(8,128)S(1)} %copy-done, f32[2,1024]{1,0:T(2,128)} %bitcast.192, ...), kind=kLoop, calls=%fused_computation.130 | loop fusion | flops 92160 | bytes 385024 | tf_op jit(solution)/shard_map/sub | solution.py:39
  86.8 7.4 %fusion.3 = f32[2,5,32,1024]{3,2,1,0:T(8,128)} fusion(f32[2,5,32,1024]{3,2,1,0:T(8,128)S(1)} %copy-done, f32[2,5,1,1024]{3,2,1,0:T(1,128)S(1)} %get-tuple-element.38, f32[2,5,31,1024]{3,2,1,0:T(8,128)} %multiply_subtract_fusion, f32[2,5,1,1024]{3,2,1,0:T(1,128)S(1)} %get-tuple-element.37, f32[2,5,32,1024]{3,2,1,0:T(8,128)} %copy-done.3, ...), kind=kLoop, calls=%fused_computation.8 | loop fusion | flops 9502720 | bytes 18128896 | tf_op jit(solution)/shard_map/sub | solution.py:184
  94.2 2.1 %dot_general.68 = f32[2,5,16,2,1024]{4,3,2,1,0:T(2,128)S(1)} reshape(f32[2,5,32,1024]{3,2,1,0:T(8,128)} %fusion.3) | data formatting | bytes 2621440 | tf_op jit(solution)/shard_map/dot_general | solution.py:186
  96.3 1.1 fusion.4
  97.6 17.3 %all-gather = f32[4,2,20480]{2,1,0:T(2,128)S(1)} all-gather(f32[1,2,20480]{2,1,0:T(2,128)S(1)} %reshape.668), channel_id=1, replica_groups=mesh['gx'=4,'gy'=4,'gz'=2] {'gx'}, dimensions={0}, use_global_device_ids=true | all-gather | bytes 819200 | tf_op jit(solution)/shard_map/all_gather | solution.py:199
  116.0 0.8 broadcast_select_fusion
  (210 shorter events, 23.3 us)
Async XLA Ops:
  3.3 34.6 %all-to-all-start = ((s32[8,1,2]{2,1,0:T(1,128)}), s32[8,1,2]{2,1,0:T(1,128)}, u32[]{:S(2)}, u32[]{:S(2)}) async-start(s32[8,1,2]{2,1,0:T(1,128)} %copy.102), calls=%async_computation | async-start | bytes 8192 | tf_op jit(solution)/shard_map/all_to_all | solution.py:131
  8.5 14.6 %copy-start.42 = (s32[32]{0:T(128)}, s32[32]{0:T(128)S(1)}, u32[]{:S(2)}) copy-start(s32[32]{0:T(128)S(1)} %broadcast_add_fusion.1) | copy-start | bytes 388
  8.5 14.6 %copy-start.40 = (s32[32]{0:T(128)}, s32[32]{0:T(128)S(1)}, u32[]{:S(2)}) copy-start(s32[32]{0:T(128)S(1)} %iota_multiply_fusion.1) | copy-start | bytes 388
  8.5 14.4 %copy-start.44 = (s32[32]{0:T(128)}, s32[32]{0:T(128)S(1)}, u32[]{:S(2)}) copy-start(s32[32]{0:T(128)S(1)} %iota_add_fusion.1) | copy-start | bytes 388
  12.7 4.0 %copy-start = (f32[2,5,32,1024]{3,2,1,0:T(8,128)S(1)}, f32[2,5,32,1024]{3,2,1,0:T(8,128)}, u32[]{:S(2)}) copy-start(f32[2,5,32,1024]{3,2,1,0:T(8,128)} %param.5) | copy-start | bytes 3932164
  20.5 1.3 %copy-start.56 = (s32[4]{0:T(128)S(1)}, s32[4]{0:T(128)}, u32[]{:S(2)}) copy-start(s32[4]{0:T(128)} %param.9) | copy-start | bytes 52
  25.7 1.2 %copy-start.14 = (f32[4,5,16,256]{3,2,1,0:T(8,128)S(1)}, f32[4,5,16,256]{3,2,1,0:T(8,128)}, u32[]{:S(2)}) copy-start(f32[4,5,16,256]{3,2,1,0:T(8,128)} %param.6) | copy-start | bytes 983044
  25.7 1.8 %copy-start.54 = (s32[16]{0:T(128)S(1)}, s32[16]{0:T(128)}, u32[]{:S(2)}) copy-start(s32[16]{0:T(128)} %iota_multiply_fusion) | copy-start | bytes 196
  28.5 2.0 %copy-start.50 = (s32[2,6]{1,0:T(2,128)S(1)}, s32[2,6]{1,0:T(2,128)}, u32[]{:S(2)}) copy-start(s32[2,6]{1,0:T(2,128)} %param.8) | copy-start | bytes 148
  28.5 1.9 %copy-start.51 = (s32[2,6]{1,0:T(2,128)S(1)}, s32[2,6]{1,0:T(2,128)}, u32[]{:S(2)}) copy-start(s32[2,6]{1,0:T(2,128)} %param.7) | copy-start | bytes 148
  28.5 2.5 %copy-start.29 = (f32[2,5,1,1024]{3,2,1,0:T(1,128)S(1)}, f32[2,5,1,1024]{3,2,1,0:T(1,128)}, u32[]{:S(2)}) copy-start(f32[2,5,1,1024]{3,2,1,0:T(1,128)} %get-tuple-element.59) | copy-start | bytes 122884
  28.6 3.1 %copy-start.8 = (f32[2,1,31,1024]{3,2,1,0:T(8,128)S(1)}, f32[2,1,31,1024]{3,2,1,0:T(8,128)}, u32[]{:S(2)}) copy-start(f32[2,1,31,1024]{3,2,1,0:T(8,128)} %get-tuple-element.28) | copy-start | bytes 761860
  34.7 1.3 %copy-start.9 = (f32[2,5,31,1024]{3,2,1,0:T(8,128)S(1)}, f32[2,5,31,1024]{3,2,1,0:T(8,128)}, u32[]{:S(2)}) copy-start(f32[2,5,31,1024]{3,2,1,0:T(8,128)} %get-tuple-element.56) | copy-start | bytes 3809284
  34.7 1.4 %copy-start.18 = (f32[2,31,1024]{2,1,0:T(8,128)S(1)}, f32[2,31,1024]{2,1,0:T(8,128)}, u32[]{:S(2)}) copy-start(f32[2,31,1024]{2,1,0:T(8,128)} %get-tuple-element.27) | copy-start | bytes 761860
  36.1 3.8 %copy-start.17 = (f32[2,8,5,1024]{3,1,2,0:T(8,128)S(1)}, f32[2,8,5,1024]{3,1,2,0:T(8,128)}, u32[]{:S(2)}) copy-start(f32[2,8,5,1024]{3,1,2,0:T(8,128)} %copy.146) | copy-start | bytes 983044
  36.1 3.8 %copy-start.53 = (s32[36]{0:T(128)S(1)}, s32[36]{0:T(128)}, u32[]{:S(2)}) copy-start(s32[36]{0:T(128)} %iota_add_fusion.2) | copy-start | bytes 436
  41.2 11.8 %all-to-all-start.1 = ((f32[8,2,5120]{2,1,0:T(2,128)}), f32[8,2,5120]{2,1,0:T(2,128)S(1)}, u32[]{:S(2)}, u32[]{:S(2)}) async-start(f32[8,2,5120]{2,1,0:T(2,128)} %reshape.665), calls=%async_computation.1 | async-start | bytes 655360 | tf_op jit(solution)/shard_map/all_to_all | solution.py:129
  45.4 7.9 %copy-start.38 = (s32[2,6]{1,0:T(2,128)S(1)}, s32[2,6]{1,0:T(2,128)}, u32[]{:S(2)}) copy-start(s32[2,6]{1,0:T(2,128)} %fusion.68) | copy-start | bytes 148
  47.4 8.6 %copy-start.23 = (f32[2,5,32,32]{3,2,1,0:T(8,128)S(1)}, f32[2,5,32,32]{3,2,1,0:T(8,128)}, u32[]{:S(2)}) copy-start(f32[2,5,32,32]{3,2,1,0:T(8,128)} %get-tuple-element.48) | copy-start | bytes 122884
  47.4 8.7 %copy-start.45 = (s32[32]{0:T(128)S(1)}, s32[32]{0:T(128)}, u32[]{:S(2)}) copy-start(s32[32]{0:T(128)} %copy-done.44) | copy-start | bytes 388
  47.4 8.7 %copy-start.49 = (pred[1024]{0:T(1024)(128)(4,1)S(1)}, pred[1024]{0:T(1024)(128)(4,1)}, u32[]{:S(2)}) copy-start(pred[1024]{0:T(1024)(128)(4,1)} %fusion.53) | copy-start | bytes 3076
  60.8 4.7 %copy-start.22 = (f32[2,5,32,1]{3,2,1,0:T(8,128)S(1)}, f32[2,5,32,1]{3,2,1,0:T(8,128)}, u32[]{:S(2)}) copy-start(f32[2,5,32,1]{3,2,1,0:T(8,128)} %get-tuple-element.54) | copy-start | bytes 3844
  60.8 4.8 %copy-start.43 = (s32[32]{0:T(128)S(1)}, s32[32]{0:T(128)}, u32[]{:S(2)}) copy-start(s32[32]{0:T(128)} %copy-done.42) | copy-start | bytes 388
  60.8 4.8 %copy-start.48 = (pred[1024]{0:T(1024)(128)(4,1)S(1)}, pred[1024]{0:T(1024)(128)(4,1)}, u32[]{:S(2)}) copy-start(pred[1024]{0:T(1024)(128)(4,1)} %fusion.47) | copy-start | bytes 3076
  64.0 1.5 %copy-start.5 = (f32[2,5,32,1023]{3,2,1,0:T(8,128)S(1)}, f32[2,5,32,1023]{3,2,1,0:T(8,128)}, u32[]{:S(2)}) copy-start(f32[2,5,32,1023]{3,2,1,0:T(8,128)} %get-tuple-element.52) | copy-start | bytes 3928324
  64.0 1.5 %copy-start.24 = (f32[2,5,32,32]{3,2,1,0:T(8,128)S(1)}, f32[2,5,32,32]{3,2,1,0:T(8,128)}, u32[]{:S(2)}) copy-start(f32[2,5,32,32]{3,2,1,0:T(8,128)} %dot_general.64) | copy-start | bytes 122884
  65.6 1.3 %copy-start.4 = (f32[2,5,32,992]{3,2,1,0:T(8,128)S(1)}, f32[2,5,32,992]{3,2,1,0:T(8,128)}, u32[]{:S(2)}) copy-start(f32[2,5,32,992]{3,2,1,0:T(8,128)} %get-tuple-element.49) | copy-start | bytes 3809284
  65.6 1.3 %copy-start.25 = (f32[2,5,32,32]{3,2,1,0:T(8,128)S(1)}, f32[2,5,32,32]{3,2,1,0:T(8,128)}, u32[]{:S(2)}) copy-start(f32[2,5,32,32]{3,2,1,0:T(8,128)} %get-tuple-element.47) | copy-start | bytes 122884
  65.6 1.3 %copy-start.26 = (f32[2,5,32,32]{3,2,1,0:T(8,128)S(1)}, f32[2,5,32,32]{3,2,1,0:T(8,128)}, u32[]{:S(2)}) copy-start(f32[2,5,32,32]{3,2,1,0:T(8,128)} %dot_general.62) | copy-start | bytes 122884
  65.6 1.3 %copy-start.47 = (pred[1024]{0:T(1024)(128)(4,1)S(1)}, pred[1024]{0:T(1024)(128)(4,1)}, u32[]{:S(2)}) copy-start(pred[1024]{0:T(1024)(128)(4,1)} %fusion.54) | copy-start | bytes 3076
  66.4 3.3 %copy-start.1 = (f32[2,5,32,1024]{3,2,1,0:T(8,128)}, f32[2,5,32,1024]{3,2,1,0:T(8,128)S(1)}, u32[]{:S(2)}) copy-start(f32[2,5,32,1024]{3,2,1,0:T(8,128)S(1)} %convolution_select_fusion.1) | copy-start | bytes 3932164
  67.4 2.1 %copy-start.2 = (f32[2,5,32,1024]{3,2,1,0:T(8,128)}, f32[2,5,32,1024]{3,2,1,0:T(8,128)S(1)}, u32[]{:S(2)}) copy-start(f32[2,5,32,1024]{3,2,1,0:T(8,128)S(1)} %convolution_select_fusion.2) | copy-start | bytes 3932164
  69.5 1.2 copy-start.12
  70.7 4.2 %copy-start.41 = (s32[32]{0:T(128)S(1)}, s32[32]{0:T(128)}, u32[]{:S(2)}) copy-start(s32[32]{0:T(128)} %copy-done.40) | copy-start | bytes 388
  70.7 4.2 %copy-start.46 = (pred[1024]{0:T(1024)(128)(4,1)S(1)}, pred[1024]{0:T(1024)(128)(4,1)}, u32[]{:S(2)}) copy-start(pred[1024]{0:T(1024)(128)(4,1)} %fusion.48) | copy-start | bytes 3076
  74.9 2.2 %copy-start.7 = (f32[2,1,32,1024]{3,2,1,0:T(8,128)S(1)}, f32[2,1,32,1024]{3,2,1,0:T(8,128)}, u32[]{:S(2)}) copy-start(f32[2,1,32,1024]{3,2,1,0:T(8,128)} %get-tuple-element.7) | copy-start | bytes 786436
  77.2 2.2 %copy-start.3 = (f32[2,5,32,1024]{3,2,1,0:T(8,128)}, f32[2,5,32,1024]{3,2,1,0:T(8,128)S(1)}, u32[]{:S(2)}) copy-start(f32[2,5,32,1024]{3,2,1,0:T(8,128)S(1)} %convolution_select_fusion) | copy-start | bytes 3932164
  79.2 1.4 %copy-start.28 = (f32[2,1,5,1024]{3,1,2,0:T(1,128)S(1)}, f32[2,1,5,1024]{3,1,2,0:T(1,128)}, u32[]{:S(2)}) copy-start(f32[2,1,5,1024]{3,1,2,0:T(1,128)} %get-tuple-element.69) | copy-start | bytes 122884
  79.3 1.4 %copy-start.31 = (f32[2,1,1024]{2,0,1:T(2,128)S(1)}, f32[2,1,1024]{2,0,1:T(2,128)}, u32[]{:S(2)}) copy-start(f32[2,1,1024]{2,0,1:T(2,128)} %get-tuple-element.94) | copy-start | bytes 24580
  79.3 1.4 %copy-start.32 = (f32[2,1,1024]{2,0,1:T(2,128)S(1)}, f32[2,1,1024]{2,0,1:T(2,128)}, u32[]{:S(2)}) copy-start(f32[2,1,1024]{2,0,1:T(2,128)} %get-tuple-element.96) | copy-start | bytes 24580
  79.3 1.4 %copy-start.33 = (f32[2,1,1024]{2,0,1:T(2,128)S(1)}, f32[2,1,1024]{2,0,1:T(2,128)}, u32[]{:S(2)}) copy-start(f32[2,1,1024]{2,0,1:T(2,128)} %get-tuple-element.97) | copy-start | bytes 24580
  79.3 1.4 %copy-start.37 = (f32[2,1,1024]{2,0,1:T(2,128)S(1)}, f32[2,1,1024]{2,0,1:T(2,128)}, u32[]{:S(2)}) copy-start(f32[2,1,1024]{2,0,1:T(2,128)} %get-tuple-element.95) | copy-start | bytes 24580
  79.4 7.4 %copy-start.19 = (f32[2,32,1024]{2,1,0:T(8,128)S(1)}, f32[2,32,1024]{2,1,0:T(8,128)}, u32[]{:S(2)}) copy-start(f32[2,32,1024]{2,1,0:T(8,128)} %get-tuple-element.6) | copy-start | bytes 786436
  79.4 7.4 %copy-start.20 = (f32[2,32,1024]{2,1,0:T(8,128)S(1)}, f32[2,32,1024]{2,1,0:T(8,128)}, u32[]{:S(2)}) copy-start(f32[2,32,1024]{2,1,0:T(8,128)} %get-tuple-element.12) | copy-start | bytes 786436
  79.4 7.4 %copy-start.21 = (f32[2,32,1024]{2,1,0:T(8,128)S(1)}, f32[2,32,1024]{2,1,0:T(8,128)}, u32[]{:S(2)}) copy-start(f32[2,32,1024]{2,1,0:T(8,128)} %get-tuple-element.64) | copy-start | bytes 786436
  94.2 2.1 %copy-start.36 = (s32[1024]{0:T(1024)S(1)}, s32[1024]{0:T(1024)}, u32[]{:S(2)}) copy-start(s32[1024]{0:T(1024)} %fusion.45) | copy-start | bytes 12292
  97.5 17.9 %copy-start.39 = (pred[4]{0:T(512)(128)(4,1)S(1)}, pred[4]{0:T(512)(128)(4,1)}, u32[]{:S(2)}) copy-start(pred[4]{0:T(512)(128)(4,1)} %broadcast_compare_fusion) | copy-start | bytes 16
  97.5 17.9 %copy-start.52 = (s32[4]{0:T(128)S(1)}, s32[4]{0:T(128)}, u32[]{:S(2)}) copy-start(s32[4]{0:T(128)} %fusion.72) | copy-start | bytes 52
  (11 other events, 10.3 us)
where the time goes:
time: 118 us; the launch traced here: 117 us
  local copies, waits for them, and re-layouts  37.5 us (32%)
  other arithmetic  35.6 us (30%)
  blocking collectives  17.3 us (15%)
  matrix products  9.61 us (8%)
  starting transfers between devices  9.36 us (8%)
  waiting for transfers between devices  5.66 us (5%)
  between operations  1.67 us (1%)
    all_gather x1, blocking collectives, body(): portion = lax.all_gather(block_rows, 'gx', axis=0, tiled=True)  17.3 us
    unnamed x124, local copies, waits for them, and re-layouts  9.93 us
    sub x1, other arithmetic, body(): updated = fine_state - courant * (step_x + step_y + step_z)  7.39 us
    unnamed x25, other arithmetic  5.83 us
    all_to_all x1, waiting for transfers between devices, body(): lax.all_to_all(lookup(lax.all_to_all(requests, ('gy', 'gz'), split_axis=0...  5.66 us
    dot_general x4, matrix products, spread(): jnp.dot(flat_layer, table, precision=highest, preferred_element_type=jnp....  5.51 us
    all_to_all x1, starting transfers between devices, body(): lax.all_to_all(requests, ('gy', 'gz'), split_axis=0, concat_axis=0, tiled...  5.17 us
    dot_general x4, local copies, waits for them, and re-layouts, spread(): jnp.dot(flat_layer, table, precision=highest, preferred_element_type=jnp....  4.95 us
  transfers between devices with their start and end apart: 2, of which 1 were waited for; matrix products, arithmetic and copies ran while one was open for 26% of the time, Pallas kernels for 0%

commit v1 on v0

v1 whole, which is shorter than its diff:
```python
import functools
import jax
import jax.numpy as jnp
from jax import lax
from jax.experimental import pallas as pl
from jax.experimental.pallas import tpu as pltpu
from jax.sharding import PartitionSpec as P

GAMMA = 5.0 / 3.0
COURANT = 0.12
LANES = 128
SUBS = 8
MESH = pl.DeviceIdType.MESH


def primitives(u):
    inverse = 1.0 / u[0]
    speeds = [u[1] * inverse, u[2] * inverse, u[3] * inverse]
    kinetic = 0.5 * (u[1] * speeds[0] + u[2] * speeds[1] + u[3] * speeds[2])
    pressure = (GAMMA - 1.0) * (u[4] - kinetic)
    square = GAMMA * pressure * inverse
    return speeds, pressure, square * lax.rsqrt(square)


def physical(u, prim, normal):
    speeds, pressure, sound = prim
    across = speeds[normal - 1]
    f = [u[normal], u[1] * across, u[2] * across, u[3] * across, (u[4] + pressure) * across]
    f[normal] = f[normal] + pressure
    return f, jnp.abs(across) + sound


def twice_flux(left, right):
    (ul, fl, sl), (ur, fr, sr) = left, right
    fastest = jnp.maximum(sl, sr)
    return [(a + b) - fastest * (d - c) for a, b, c, d in zip(fl, fr, ul, ur)]


def moved(u, f, s, normal, move):
    ud = [move(x) for x in u]
    fd = [ud[normal] if k == 0 else move(f[k]) for k in range(5)]
    return ud, fd, move(s)


def split_dot(x, table, terms):
    total = None
    for term in range(terms):
        part = x.astype(jnp.bfloat16)
        if term < terms - 1:
            x = x - part.astype(jnp.float32)
        add = jnp.dot(part, table, preferred_element_type=jnp.float32)
        total = add if total is None else total + add
    return total


def iota(shape, dim):
    return lax.broadcasted_iota(jnp.int32, shape, dim)


def lane_total(x):
    for shift in (1, 2, 4, 8, 16, 32, 64):
        x = x + pltpu.roll(x, shift, 1)
    return x


def kernel(
    dims,
    fine_hbm, coarse_hbm, neigh, csrc, cov,
    fine_out, coarse_out,
    fine, coarse, nxt_state, table, widened, rows_y, flux_d, restr, coarse_next,
    ids, req_send, req_recv, reqx_send, reqx_recv, rep_send, replies, rx_send, rx_recv,
    in_sem, out_sem, req_ss, req_rs, reqx_ss, reqx_rs, rep_ss, rep_rs, rx_ss, rx_rs,
):
    line, columns, gz_size, boxes, blocks, edge, half, slots = dims
    f32, i32 = jnp.float32, jnp.int32
    plane = edge * edge
    tiles = plane // LANES
    quarters = edge // SUBS
    faces = boxes * 6
    per_tile = LANES // edge
    gx = lax.axis_index("gx")
    gy = lax.axis_index("gy")
    gz = lax.axis_index("gz")
    me = gy * gz_size + gz

    def line_dev(p):
        return (gx, lax.div(p, gz_size), lax.rem(p, gz_size))

    def col_dev(x):
        return (x, gy, gz)

    load_fine = pltpu.make_async_copy(fine_hbm, fine, in_sem.at[0])
    load_coarse = pltpu.make_async_copy(coarse_hbm, coarse, in_sem.at[1])
    load_fine.start()
    load_coarse.start()

    barrier = pltpu.get_barrier_semaphore()
    for d in range(1, line):
        pl.semaphore_signal(barrier, 1, device_id=line_dev(lax.rem(me + d, line)), device_id_type=MESH)
    for d in range(1, columns):
        pl.semaphore_signal(barrier, 1, device_id=col_dev(lax.rem(gx + d, columns)), device_id_type=MESH)

    ids[...] = jnp.full((24, LANES), -1, i32)
    ids[0:boxes, 0:6] = neigh[...]
    ids[8 : 8 + boxes, 0:6] = csrc[...]
    ids[16:17, 0:blocks] = cov[...]
    lane8 = iota((SUBS, LANES), 1)
    sub8 = iota((SUBS, LANES), 0)

    def in_row(tile):
        row = tile[0:1, :]
        for b in range(1, boxes):
            lane1 = lane8[0:1, :]
            row = jnp.where(lane1 >= 6 * b, pltpu.roll(tile, 6 * b, 1)[b : b + 1, :], row)
        return jnp.broadcast_to(row, (line, LANES))

    lane = iota((line, LANES), 1)
    sub = iota((line, LANES), 0)
    near = in_row(ids[0:8, :])
    far = in_row(ids[8:16, :])
    is_fine = near >= 0
    near_dev = lax.div(near, jnp.full_like(near, boxes))
    far_dev = lax.div(far, jnp.full_like(far, blocks))
    side = lane
    for b in range(1, boxes):
        side = jnp.where(lane >= 6 * b, lane - 6 * b, side)
    facing = jnp.bitwise_xor(side, 1)
    code = jnp.where(
        is_fine,
        (near - near_dev * boxes) * 6 + facing,
        faces + (far - far_dev * blocks) * 6 + facing,
    )
    away = jnp.where(is_fine, near_dev, far_dev) - gx * line - me
    away = jnp.where(away < 0, away + line, away)
    match = (away == sub) & (lane < faces)
    ones = jnp.where(match, 1, 0)
    run = ones
    for shift in (1, 2, 4, 8):
        run = run + jnp.where(lane >= shift, pltpu.roll(run, shift, 1), 0)
    rank = run - ones
    asked = jnp.zeros((line, LANES), i32)
    for k in range(slots):
        asked = jnp.where(lane == k, lane_total(jnp.where(match & (rank == k), code, 0)), asked)
    for d in range(line):
        req_send[d] = jnp.broadcast_to(asked[d : d + 1, :], (SUBS, LANES))
    place = jnp.where(match & (rank < slots), sub * slots + rank, 0)
    place_tile = place[0:SUBS, :]
    for part in range(1, line // SUBS):
        place_tile = place_tile + place[part * SUBS : (part + 1) * SUBS, :]
    for shift in (1, 2, 4):
        place_tile = place_tile + pltpu.roll(place_tile, shift, 0)

    cover = jnp.broadcast_to(ids[16:17, :], (SUBS, LANES))
    cover_dev = lax.div(cover, jnp.full_like(cover, boxes))
    cover_col = lax.div(cover_dev, jnp.full_like(cover, line)) - gx
    cover_col = jnp.where(cover_col < 0, cover_col + columns, cover_col)
    covered = cover >= 0
    wanted = lane_total(
        jnp.where(covered & (cover_col == sub8), cover - cover_dev * boxes, 0)
    )
    for d in range(columns):
        reqx_send[d] = jnp.broadcast_to(wanted[d : d + 1, :], (SUBS, LANES))
    cover_col = jnp.where(covered, cover_col, 0)
    covered = jnp.where(covered, 1, 0)

    pl.semaphore_wait(barrier, line - 1 + columns - 1)

    req_copies = {}
    for d in range(1, line):
        req_copies[d] = pltpu.make_async_remote_copy(
            req_send.at[d], req_recv.at[d], req_ss.at[d], req_rs.at[d],
            device_id=line_dev(lax.rem(me + d, line)), device_id_type=MESH,
        )
        req_copies[d].start()
    reqx_copies = {}
    for d in range(1, columns):
        reqx_copies[d] = pltpu.make_async_remote_copy(
            reqx_send.at[d], reqx_recv.at[d], reqx_ss.at[d], reqx_rs.at[d],
            device_id=col_dev(lax.rem(gx + d, columns)), device_id_type=MESH,
        )
        reqx_copies[d].start()

    def tile_at(t):
        return pl.ds(t * LANES, LANES)

    in_edge = lane8 & (edge - 1)
    group = lane8 // edge
    load_fine.wait()

    def fine_layers(bc, carry):
        b = lax.div(bc, 5)
        c = bc - b * 5
        row = pl.multiple_of(bc * edge, edge)
        z_low = jnp.zeros((SUBS, LANES), f32)
        z_high = jnp.zeros((SUBS, LANES), f32)
        y_low = jnp.zeros((SUBS, LANES), f32)
        y_high = jnp.zeros((SUBS, LANES), f32)
        for q in range(quarters):
            for t in range(tiles):
                block = fine[pl.ds(row + q * SUBS, SUBS), tile_at(t)]
                s = q * SUBS + t
                z_low = jnp.where(in_edge == s, pltpu.roll(block, s, 1), z_low)
                z_high = jnp.where(in_edge == s, pltpu.roll(block, (s - edge + 1) % LANES, 1), z_high)
                if t == 0:
                    y_low = jnp.where(group == q, pltpu.roll(block, q * edge, 1), y_low)
                if t == tiles - 1:
                    y_high = jnp.where(
                        group == q, pltpu.roll(block, (q * edge - (LANES - edge)) % LANES, 1), y_high
                    )
                if q == 0:
                    table[b * 6, c, t : t + 1, :] = block[0:1, :]
                if q == quarters - 1:
                    table[b * 6 + 1, c, t : t + 1, :] = block[SUBS - 1 : SUBS, :]
        table[b * 6 + 2, c] = y_low
        table[b * 6 + 3, c] = y_high
        table[b * 6 + 4, c] = z_low
        table[b * 6 + 5, c] = z_high
        return carry

    lax.fori_loop(0, boxes * 5, fine_layers, 0)

    load_coarse.wait()
    small = half * half
    src = iota((small, 2 * LANES), 0)
    col = iota((small, 2 * LANES), 1)
    lane_w = col & (LANES - 1)
    y_src = (lane_w // edge) * ((half - 1) * half) + (lane_w & (edge - 1)) // 2
    z_j = 4 * (lane_w & (SUBS - 1)) + lane_w // edge
    z_src = (z_j // 2) * half + ((lane_w & (edge - 1)) // SUBS) * (half - 1)
    y_ok = (col < LANES) & (lane_w < 2 * edge) & (src == y_src)
    z_ok = (col >= LANES) & ((lane_w & (edge - 1)) < 2 * SUBS) & (src == z_src)
    lateral_table = jnp.where(y_ok | z_ok, 1.0, 0.0).astype(jnp.bfloat16)
    lateral = split_dot(coarse[...], lateral_table, 3)
    rows = blocks * 5 * half
    for part in range(2):
        piece = lateral[:, part * LANES : (part + 1) * LANES]
        widened[part, pl.ds(0, rows, stride=2), :] = piece
        widened[part, pl.ds(1, rows, stride=2), :] = piece
    z_group = in_edge // SUBS

    def coarse_layers(bc, carry):
        b = lax.div(bc, 5)
        c = bc - b * 5
        row = pl.multiple_of(bc * edge, edge)
        for f in range(2):
            y = jnp.zeros((SUBS, LANES), f32)
            z = jnp.zeros((SUBS, LANES), f32)
            for q in range(quarters):
                block = widened[0, pl.ds(row + q * SUBS, SUBS), :]
                y = jnp.where(group == q, pltpu.roll(block, (edge * (q - f)) % LANES, 1), y)
                block = widened[1, pl.ds(row + q * SUBS, SUBS), :]
                z = jnp.where(z_group == q, pltpu.roll(block, (SUBS * (q - f)) % LANES, 1), z)
            x = jnp.zeros((SUBS, LANES), f32)
            at = pl.multiple_of(bc * half, half)
            for t in range(SUBS):
                block = coarse[pl.ds(at + f * (half - SUBS), SUBS), tile_at(t // 4)]
                line_row = block[f * (SUBS - 1) : f * (SUBS - 1) + 1, :]
                line_row = jnp.broadcast_to(line_row, (SUBS, LANES))
                x = jnp.where(sub8 == t, pltpu.roll(line_row, (-2 * half * (t % 4)) % LANES, 1), x)
            rows_y[f, pl.ds(pl.multiple_of(bc * SUBS, SUBS), SUBS), :] = x
            table[faces + b * 6 + 2 + f, c] = y
            table[faces + b * 6 + 4 + f, c] = z
        return carry

    lax.fori_loop(0, blocks * 5, coarse_layers, 0)

    src = iota((LANES, LANES), 0)
    col = iota((LANES, LANES), 1)
    x_table = jnp.where(
        src == (col // (2 * edge)) * half + (col & (edge - 1)) // 2, 1.0, 0.0
    ).astype(jnp.bfloat16)
    for f in range(2):
        spread = split_dot(rows_y[f], x_table, 3)
        for b in range(blocks):
            for c in range(5):
                at = (b * 5 + c) * SUBS
                table[faces + b * 6 + f, c] = spread[at : at + SUBS, :]

    my_codes = asked[0:1, :]
    rep_copies = {}
    for d in list(range(1, line)) + [0]:
        if d:
            req_copies[d].wait_recv()
            codes = req_recv[d][0:1, :]
        else:
            codes = my_codes
        for k in range(slots):
            layer = table[codes[0, k]]
            if d:
                rep_send[d, k] = layer
            else:
                replies[d * slots + k] = layer
        if d:
            rep_copies[d] = pltpu.make_async_remote_copy(
                rep_send.at[d], replies.at[pl.ds(d * slots, slots)], rep_ss.at[d], rep_rs.at[d],
                device_id=line_dev(lax.rem(me + line - d, line)), device_id_type=MESH,
            )
            rep_copies[d].start()

    tall_lane = iota((edge, LANES), 1)
    tall_row = iota((edge, LANES), 0)
    not_last_x = tall_row < edge - 1
    not_last_z = (tall_lane & (edge - 1)) < edge - 1

    def box_step(b, carry):
        def load(t):
            return [
                fine[pl.ds(pl.multiple_of((b * 5 + c) * edge, edge), edge), tile_at(t)]
                for c in range(5)
            ]

        cur = load(0)
        prim = primitives(cur)
        before = [jnp.zeros((edge, LANES), f32)] * 5
        for t in range(tiles):
            if t < tiles - 1:
                after = load(t + 1)
                after_prim = primitives(after)
            else:
                after, after_prim = cur, prim
            f, s = physical(cur, prim, 1)
            right = moved(cur, f, s, 1, lambda x: pltpu.roll(x, edge - 1, 0))
            flux = [jnp.where(not_last_x, x, 0.0) for x in twice_flux((cur, f, s), right)]
            step = [x - pltpu.roll(x, 1, 0) for x in flux]
            f, s = physical(cur, prim, 3)
            right = moved(cur, f, s, 3, lambda x: pltpu.roll(x, LANES - 1, 1))
            flux = [jnp.where(not_last_z, x, 0.0) for x in twice_flux((cur, f, s), right)]
            step = [a + (x - pltpu.roll(x, 1, 1)) for a, x in zip(step, flux)]
            f, s = physical(cur, prim, 2)
            fa, sa = physical(after, after_prim, 2)

            def up(here, there):
                return pltpu.roll(jnp.where(tall_lane < edge, there, here), LANES - edge, 1)

            ud = [up(x, y) for x, y in zip(cur, after)]
            fd = [ud[2]] + [up(x, y) for x, y in zip(f[1:], fa[1:])]
            flux = twice_flux((cur, f, s), (ud, fd, up(s, sa)))
            if t == tiles - 1:
                flux = [jnp.where(tall_lane < LANES - edge, x, 0.0) for x in flux]
            for c in range(5):
                low = pltpu.roll(
                    jnp.where(tall_lane >= LANES - edge, before[c], flux[c]), edge, 1
                )
                total = step[c] + (flux[c] - low)
                nxt_state[t, pl.ds(pl.multiple_of((b * 5 + c) * edge, edge), edge), :] = (
                    cur[c] - (0.5 * COURANT) * total
                )
            before = flux
            cur, prim = after, after_prim
        return carry

    lax.fori_loop(0, boxes, box_step, 0)

    src = iota((4 * LANES, LANES), 0)
    col = iota((4 * LANES, LANES), 1)
    shrink = jnp.where(
        ((src // (2 * edge)) == col // half) & ((src & (edge - 1)) // 2 == (col & (half - 1))),
        0.125,
        0.0,
    ).astype(jnp.bfloat16)

    for d in range(1, line):
        rep_copies[d].wait_recv()
    for b in range(boxes):
        for g in range(6):
            ghost_all = replies[place_tile[0:1, :][0, b * 6 + g]]
            own_all = table[b * 6 + g]
            normal = g // 2 + 1
            pair = []
            for layers in (ghost_all, own_all):
                u = [layers[c] for c in range(5)]
                pair.append((u,) + physical(u, primitives(u), normal))
            if g % 2:
                flux = twice_flux(pair[1], pair[0])
                scale = -0.5 * COURANT
            else:
                flux = twice_flux(pair[0], pair[1])
                scale = 0.5 * COURANT
            for c in range(5):
                flux_d[b * 6 + g, c] = scale * flux[c]

    def add_faces(bc, carry):
        b = lax.div(bc, 5)
        c = bc - b * 5
        row = pl.multiple_of(bc * edge, edge)
        d = [flux_d[b * 6 + g, c] for g in range(6)]
        for q in range(quarters):
            for t in range(tiles):
                s = q * SUBS + t
                at = (t, pl.ds(row + q * SUBS, SUBS), slice(None))
                block = nxt_state[at]
                block = block + jnp.where(
                    in_edge == 0,
                    pltpu.roll(d[4], (-s) % LANES, 1),
                    jnp.where(in_edge == edge - 1, pltpu.roll(d[5], (edge - 1 - s) % LANES, 1), 0.0),
                )
                if t == 0:
                    block = block + jnp.where(group == 0, pltpu.roll(d[2], (-q * edge) % LANES, 1), 0.0)
                if t == tiles - 1:
                    block = block + jnp.where(
                        group == per_tile - 1,
                        pltpu.roll(d[3], (LANES - edge - q * edge) % LANES, 1),
                        0.0,
                    )
                if q == 0:
                    block = block + jnp.where(sub8 == 0, d[0][t : t + 1, :], 0.0)
                if q == quarters - 1:
                    block = block + jnp.where(sub8 == SUBS - 1, d[1][t : t + 1, :], 0.0)
                nxt_state[at] = block
        return carry

    lax.fori_loop(0, boxes * 5, add_faces, 0)

    stores = []
    for t in range(tiles):
        stores.append(
            pltpu.make_async_copy(nxt_state.at[t], fine_out.at[:, tile_at(t)], out_sem.at[1 + t])
        )
        stores[-1].start()

    for h in range(2):
        parts = []
        for t in range(4 * h, 4 * h + 4):
            parts.append(
                nxt_state[t, pl.ds(0, boxes * 5 * half, stride=2), :]
                + nxt_state[t, pl.ds(1, boxes * 5 * half, stride=2), :]
            )
        mean = split_dot(jnp.concatenate(parts, axis=1), shrink, 2)
        for b in range(boxes):
            restr[b, :, tile_at(h)] = mean[b * 5 * half : (b + 1) * 5 * half, :]

    rx_copies = {}
    for d in list(range(1, columns)) + [0]:
        if d:
            reqx_copies[d].wait_recv()
            which = reqx_recv[d][0:1, :][0, 0]
            rx_send[d] = restr[which]
            rx_copies[d] = pltpu.make_async_remote_copy(
                rx_send.at[d], rx_recv.at[d], rx_ss.at[d], rx_rs.at[d],
                device_id=col_dev(lax.rem(gx + columns - d, columns)), device_id_type=MESH,
            )
            rx_copies[d].start()
        else:
            rx_recv[0] = restr[wanted[0:1, :][0, 0]]
    for d in range(1, columns):
        rx_copies[d].wait_recv()
    for c in range(blocks):
        part = pl.ds(c * 5 * half, 5 * half)
        flag = covered[0:1, :][0, c]
        coarse_next[part, :] = jnp.where(flag > 0, rx_recv[cover_col[0:1, :][0, c]], coarse[part, :])
    store_coarse = pltpu.make_async_copy(coarse_next, coarse_out, out_sem.at[0])
    store_coarse.start()

    for copies in (req_copies, reqx_copies, rep_copies, rx_copies):
        for d in copies:
            copies[d].wait_send()
    for store in stores:
        store.wait()
    store_coarse.wait()


def body(fine_state, coarse_state, neighbours, coarse_sources, covering):
    boxes, comps, edge, plane = fine_state.shape
    blocks, _, half, small = coarse_state.shape
    line = lax.axis_size("gy") * lax.axis_size("gz")
    columns = lax.axis_size("gx")
    faces = boxes * 6
    slots = -(-faces // line)
    dims = (line, columns, lax.axis_size("gz"), boxes, blocks, edge, half, slots)
    fine_rows = boxes * comps * edge
    coarse_rows = blocks * comps * half
    f32, i32 = jnp.float32, jnp.int32
    vmem = pltpu.VMEM
    dma = pltpu.SemaphoreType.DMA
    layer = (comps, SUBS, LANES)
    fine_next, coarse_next = pl.pallas_call(
        functools.partial(kernel, dims),
        out_shape=(
            jax.ShapeDtypeStruct((fine_rows, plane), f32),
            jax.ShapeDtypeStruct((coarse_rows, small), f32),
        ),
        in_specs=[pl.BlockSpec(memory_space=pl.ANY)] * 2
        + [pl.BlockSpec(memory_space=pltpu.VMEM)] * 3,
        out_specs=(pl.BlockSpec(memory_space=pl.ANY),) * 2,
        scratch_shapes=[
            vmem((fine_rows, plane), f32),
            vmem((coarse_rows, small), f32),
            vmem((plane // LANES, fine_rows, LANES), f32),
            vmem((faces + 6 * blocks,) + layer, f32),
            vmem((2, 2 * coarse_rows, LANES), f32),
            vmem((2, blocks * comps * SUBS, LANES), f32),
            vmem((faces,) + layer, f32),
            vmem((boxes, comps * half, small), f32),
            vmem((coarse_rows, small), f32),
            vmem((24, LANES), i32),
            vmem((line, SUBS, LANES), i32),
            vmem((line, SUBS, LANES), i32),
            vmem((columns, SUBS, LANES), i32),
            vmem((columns, SUBS, LANES), i32),
            vmem((line, slots) + layer, f32),
            vmem((line * slots,) + layer, f32),
            vmem((columns, comps * half, small), f32),
            vmem((columns, comps * half, small), f32),
            dma((2,)),
            dma((1 + plane // LANES,)),
        ]
        + [dma((line,)), dma((line,)), dma((columns,)), dma((columns,))]
        + [dma((line,)), dma((line,)), dma((columns,)), dma((columns,))],
        compiler_params=pltpu.CompilerParams(
            collective_id=0, has_side_effects=True, vmem_limit_bytes=40 * 1024 * 1024
        ),
    )(
        fine_state.reshape(fine_rows, plane),
        coarse_state.reshape(coarse_rows, small),
        neighbours,
        coarse_sources,
        covering.reshape(1, blocks),
    )
    return fine_next.reshape(fine_state.shape), coarse_next.reshape(coarse_state.shape)


def solution(mesh):
    spec = ("gx", "gy", "gz")
    wide = P(spec, None, None, None)
    return jax.shard_map(
        body,
        mesh=mesh,
        in_specs=(wide, wide, P(spec, None), P(spec, None), P(spec)),
        out_specs=(wide, wide),
        check_vma=False,
    )
```

time: 118 us -> 33.8 us (0.29)
  other arithmetic: 35.6 us -> 0 us
  local copies, waits for them, and re-layouts: 37.5 us -> 6.08 us
  Pallas kernels: 0 us -> 26.8 us
  blocking collectives: 17.3 us -> 0 us
  matrix products: 9.61 us -> 0 us
  starting transfers between devices: 9.36 us -> 0 us
  waiting for transfers between devices: 5.66 us -> 0 us
    pallas_call x0 -> x1, Pallas kernels: none -> 26.8 us  [body(): pl.pallas_call(functools.partial(kernel, dims), out_shape=(jax.ShapeDtype...]
    all_gather x1 -> x0, blocking collectives: 17.3 us -> none  [body(): portion = lax.all_gather(block_rows, 'gx', axis=0, tiled=True)]
    slice x10 -> x0, local copies, waits for them, and re-layouts: 11.5 us -> none  [the longest x2 4.77 us: body(): jnp.roll(fine_state, edge_cells, axis=3)]
    sub x5 -> x0, other arithmetic: 10.3 us -> none  [the longest x1 7.39 us: body(): updated = fine_state - courant * (step_x + step_y + step_z)]
    dot_general x11 -> x0, matrix products: 9.61 us -> none  [the longest x4 5.51 us: spread(): jnp.dot(flat_layer, table, precision=highest, preferred_element_type=jnp....]
    all_to_all x2 -> x0, starting transfers between devices: 9.36 us -> none  [the longest x1 5.17 us: body(): lax.all_to_all(requests, ('gy', 'gz'), split_axis=0, concat_axis=0, tiled...]
    dot_general x6 -> x0, local copies, waits for them, and re-layouts: 7.12 us -> none  [the longest x4 4.95 us: spread(): jnp.dot(flat_layer, table, precision=highest, preferred_element_type=jnp....]
    unnamed x25 -> x0, other arithmetic: 5.83 us -> none
  transfers between devices with their start and end apart: 2 -> 0, of which waited for: 1 -> 0; matrix products, arithmetic and copies ran while one was open for 26% -> 0% of each run, Pallas kernels for 0% -> 0%
where the time goes in v1:
time: 33.8 us; the launch traced here: 33.5 us
  Pallas kernels  26.8 us (79%)
  local copies, waits for them, and re-layouts  6.08 us (18%)
  between operations  0.65 us (2%)
    pallas_call x1, Pallas kernels, body(): pl.pallas_call(functools.partial(kernel, dims), out_shape=(jax.ShapeDtype...  26.8 us
    unnamed x12, local copies, waits for them, and re-layouts  6.08 us

profile of v1, /device:TPU:0, one launch (start us, length us, event | category | flops | bytes accessed | tf_op | source)
XLA Modules:
  0.0 33.5 jit_solution(2240964704555438745)
XLA Ops:
  0.6 0.0 copy-start
  0.6 1.3 %copy-done = f32[2,5,32,1024]{3,2,1,0:T(8,128)S(1)} copy-done((f32[2,5,32,1024]{3,2,1,0:T(8,128)S(1)}, f32[2,5,32,1024]{3,2,1,0:T(8,128)}, u32[]{:S(2)}) %copy-start) | copy-done | bytes 1310744
  1.9 0.0 copy-start.1
  2.0 1.0 %copy-done.1 = f32[4,5,16,256]{3,2,1,0:T(8,128)S(1)} copy-done((f32[4,5,16,256]{3,2,1,0:T(8,128)S(1)}, f32[4,5,16,256]{3,2,1,0:T(8,128)}, u32[]{:S(2)}) %copy-start.1) | copy-done | bytes 327704
  2.9 0.0 copy-start.2
  2.9 0.7 %copy-done.2 = s32[2,6]{1,0:T(2,128)S(1)} copy-done((s32[2,6]{1,0:T(2,128)S(1)}, s32[2,6]{1,0:T(2,128)}, u32[]{:S(2)}) %copy-start.2) | copy-done | bytes 72
  3.6 0.0 copy-start.3
  3.6 0.7 %copy-done.3 = s32[2,6]{1,0:T(2,128)S(1)} copy-done((s32[2,6]{1,0:T(2,128)S(1)}, s32[2,6]{1,0:T(2,128)}, u32[]{:S(2)}) %copy-start.3) | copy-done | bytes 72
  4.3 0.0 copy-start.4
  4.3 0.7 %copy-done.4 = s32[4]{0:T(128)S(1)} copy-done((s32[4]{0:T(128)S(1)}, s32[4]{0:T(128)}, u32[]{:S(2)}) %copy-start.4) | copy-done | bytes 40
  4.9 26.8 %shard_map.68 = (f32[320,1024]{1,0:T(8,128)S(1)}, f32[320,256]{1,0:T(8,128)S(1)}) custom-call(f32[320,1024]{1,0:T(8,128)S(1)} %bitcast.5, f32[320,256]{1,0:T(8,128)S(1)} %bitcast.8, s32[2,6]{1,0:T(2,128)S(1)} %copy-done.2, s32[2,6]{1,0:T(2,128)S(1)} %copy-done.3, s32[1,4]{1,0:T(1,128)S(1)} %bitcast.9), custom_call_target="tpu_custom_call" | custom-call | tf_op jit(solution)/shard_map/pallas_call | solution.py:476
  31.7 1.1 %copy.9 = f32[2,5,32,1024]{3,2,1,0:T(8,128)} copy(f32[2,5,32,1024]{3,2,1,0:T(8,128)S(1)} %bitcast.6) | data formatting | bytes 2621440
  32.8 0.7 %copy.10 = f32[4,5,16,256]{3,2,1,0:T(8,128)} copy(f32[4,5,16,256]{3,2,1,0:T(8,128)S(1)} %bitcast.7) | data formatting | bytes 655360
Async XLA Ops:
  0.6 1.3 %copy-start = (f32[2,5,32,1024]{3,2,1,0:T(8,128)S(1)}, f32[2,5,32,1024]{3,2,1,0:T(8,128)}, u32[]{:S(2)}) copy-start(f32[2,5,32,1024]{3,2,1,0:T(8,128)} %param.5) | copy-start | bytes 3932164
  1.9 1.0 %copy-start.1 = (f32[4,5,16,256]{3,2,1,0:T(8,128)S(1)}, f32[4,5,16,256]{3,2,1,0:T(8,128)}, u32[]{:S(2)}) copy-start(f32[4,5,16,256]{3,2,1,0:T(8,128)} %param.6) | copy-start | bytes 983044
  2.9 0.7 %copy-start.2 = (s32[2,6]{1,0:T(2,128)S(1)}, s32[2,6]{1,0:T(2,128)}, u32[]{:S(2)}) copy-start(s32[2,6]{1,0:T(2,128)} %neigh.1) | copy-start | bytes 148
  3.6 0.7 %copy-start.3 = (s32[2,6]{1,0:T(2,128)S(1)}, s32[2,6]{1,0:T(2,128)}, u32[]{:S(2)}) copy-start(s32[2,6]{1,0:T(2,128)} %csrc.1) | copy-start | bytes 148
  4.3 0.7 %copy-start.4 = (s32[4]{0:T(128)S(1)}, s32[4]{0:T(128)}, u32[]{:S(2)}) copy-start(s32[4]{0:T(128)} %param.9) | copy-start | bytes 52

commit v2 on v1

--- a/solution.py
+++ b/solution.py
@@ -65,10 +65,10 @@
 
 def kernel(
     dims,
-    fine_hbm, coarse_hbm, neigh, csrc, cov,
+    fine_hbm, coarse_hbm, neigh_hbm, csrc_hbm, cov_hbm,
     fine_out, coarse_out,
     fine, coarse, nxt_state, table, widened, rows_y, flux_d, restr, coarse_next,
-    ids, req_send, req_recv, reqx_send, reqx_recv, rep_send, replies, rx_send, rx_recv,
+    neigh, csrc, cov, ids, req_send, req_recv, reqx_send, reqx_recv, rep_send, replies, rx_send, rx_recv,
     in_sem, out_sem, req_ss, req_rs, reqx_ss, reqx_rs, rep_ss, rep_rs, rx_ss, rx_rs,
 ):
     line, columns, gz_size, boxes, blocks, edge, half, slots = dims
@@ -91,6 +91,12 @@
 
     load_fine = pltpu.make_async_copy(fine_hbm, fine, in_sem.at[0])
     load_coarse = pltpu.make_async_copy(coarse_hbm, coarse, in_sem.at[1])
+    load_ids = [
+        pltpu.make_async_copy(a, b, in_sem.at[2 + i])
+        for i, (a, b) in enumerate(((neigh_hbm, neigh), (csrc_hbm, csrc), (cov_hbm, cov)))
+    ]
+    for load in load_ids:
+        load.start()
     load_fine.start()
     load_coarse.start()
 
@@ -100,6 +106,8 @@
     for d in range(1, columns):
         pl.semaphore_signal(barrier, 1, device_id=col_dev(lax.rem(gx + d, columns)), device_id_type=MESH)
 
+    for load in load_ids:
+        load.wait()
     ids[...] = jnp.full((24, LANES), -1, i32)
     ids[0:boxes, 0:6] = neigh[...]
     ids[8 : 8 + boxes, 0:6] = csrc[...]
@@ -479,8 +487,7 @@
             jax.ShapeDtypeStruct((fine_rows, plane), f32),
             jax.ShapeDtypeStruct((coarse_rows, small), f32),
         ),
-        in_specs=[pl.BlockSpec(memory_space=pl.ANY)] * 2
-        + [pl.BlockSpec(memory_space=pltpu.VMEM)] * 3,
+        in_specs=[pl.BlockSpec(memory_space=pl.ANY)] * 5,
         out_specs=(pl.BlockSpec(memory_space=pl.ANY),) * 2,
         scratch_shapes=[
             vmem((fine_rows, plane), f32),
@@ -492,6 +499,9 @@
             vmem((faces,) + layer, f32),
             vmem((boxes, comps * half, small), f32),
             vmem((coarse_rows, small), f32),
+            vmem((boxes, 6), i32),
+            vmem((boxes, 6), i32),
+            vmem((1, blocks), i32),
             vmem((24, LANES), i32),
             vmem((line, SUBS, LANES), i32),
             vmem((line, SUBS, LANES), i32),
@@ -501,13 +511,13 @@
             vmem((line * slots,) + layer, f32),
             vmem((columns, comps * half, small), f32),
             vmem((columns, comps * half, small), f32),
-            dma((2,)),
+            dma((5,)),
             dma((1 + plane // LANES,)),
         ]
         + [dma((line,)), dma((line,)), dma((columns,)), dma((columns,))]
         + [dma((line,)), dma((line,)), dma((columns,)), dma((columns,))],
         compiler_params=pltpu.CompilerParams(
-            collective_id=0, has_side_effects=True, vmem_limit_bytes=40 * 1024 * 1024
+            collective_id=0, has_side_effects=True, vmem_limit_bytes=62 * 1024 * 1024
         ),
     )(
         fine_state.reshape(fine_rows, plane),

time: 33.8 us -> 31.3 us (0.926)
  local copies, waits for them, and re-layouts: 6.08 us -> 3.3 us
  Pallas kernels: 26.8 us -> 27.2 us
    unnamed x12 -> x4, local copies, waits for them, and re-layouts: 6.08 us -> 3.3 us
    pallas_call x1, Pallas kernels: 26.8 us -> 27.2 us  [body(): pl.pallas_call(functools.partial(kernel, dims), out_shape=(jax.ShapeDtype...]
where the time goes in v2:
time: 31.3 us; the launch traced here: 31.2 us
  Pallas kernels  27.2 us (87%)
  local copies, waits for them, and re-layouts  3.3 us (11%)
  between operations  0.65 us (2%)
    pallas_call x1, Pallas kernels, body(): pl.pallas_call(functools.partial(kernel, dims), out_shape=(jax.ShapeDtype...  27.2 us
    unnamed x4, local copies, waits for them, and re-layouts  3.3 us

profile of v2, /device:TPU:0, one launch (start us, length us, event | category | flops | bytes accessed | tf_op | source)
XLA Modules:
  0.0 31.2 jit_solution(13790377705556780462)
XLA Ops:
  0.6 27.2 %shard_map.68 = (f32[320,1024]{1,0:T(8,128)}, f32[320,256]{1,0:T(8,128)}) custom-call(f32[320,1024]{1,0:T(8,128)} %bitcast.5, f32[320,256]{1,0:T(8,128)} %bitcast.8, s32[2,6]{1,0:T(2,128)} %neigh_hbm.1, s32[2,6]{1,0:T(2,128)} %csrc_hbm.1, s32[1,4]{1,0:T(1,128)} %bitcast.9), custom_call_target="tpu_custom_call" | custom-call | tf_op jit(solution)/shard_map/pallas_call | solution.py:484
  27.9 0.0 copy-start
  27.9 2.6 %copy.9 = f32[2,5,32,1024]{3,2,1,0:T(8,128)} copy(f32[2,5,32,1024]{3,2,1,0:T(8,128)} %bitcast.6) | data formatting | bytes 2621440
  30.4 0.0 copy-done
  30.4 0.7 %copy.10 = f32[4,5,16,256]{3,2,1,0:T(8,128)} copy(f32[4,5,16,256]{3,2,1,0:T(8,128)S(1)} %bitcast.7) | data formatting | bytes 655360
Async XLA Ops:
  27.9 2.6 %copy-start = (f32[320,256]{1,0:T(8,128)S(1)}, f32[320,256]{1,0:T(8,128)}, u32[]{:S(2)}) copy-start(f32[320,256]{1,0:T(8,128)} %get-tuple-element.5) | copy-start | bytes 983044

commit v3 on v2

--- a/solution.py
+++ b/solution.py
@@ -69,6 +69,7 @@
     fine_out, coarse_out,
     fine, coarse, nxt_state, table, widened, rows_y, flux_d, restr, coarse_next,
     neigh, csrc, cov, ids, req_send, req_recv, reqx_send, reqx_recv, rep_send, replies, rx_send, rx_recv,
+    carried, pooled, pool_send, pool_recv,
     in_sem, out_sem, req_ss, req_rs, reqx_ss, reqx_rs, rep_ss, rep_rs, rx_ss, rx_rs,
 ):
     line, columns, gz_size, boxes, blocks, edge, half, slots = dims
@@ -305,22 +306,34 @@
             )
             rep_copies[d].start()
 
+    src = iota((4 * LANES, LANES), 0)
+    col = iota((4 * LANES, LANES), 1)
+    shrink = jnp.where(
+        ((src // (2 * edge)) == col // half) & ((src & (edge - 1)) // 2 == (col & (half - 1))),
+        0.125,
+        0.0,
+    ).astype(jnp.bfloat16)
+
     tall_lane = iota((edge, LANES), 1)
     tall_row = iota((edge, LANES), 0)
     not_last_x = tall_row < edge - 1
     not_last_z = (tall_lane & (edge - 1)) < edge - 1
 
-    def box_step(b, carry):
+    def box_step(half_box, b):
         def load(t):
             return [
                 fine[pl.ds(pl.multiple_of((b * 5 + c) * edge, edge), edge), tile_at(t)]
                 for c in range(5)
             ]
 
-        cur = load(0)
+        first = half_box * (tiles // 2)
+        cur = load(first)
         prim = primitives(cur)
-        before = [jnp.zeros((edge, LANES), f32)] * 5
-        for t in range(tiles):
+        if half_box:
+            before = [carried[b, c] for c in range(5)]
+        else:
+            before = [jnp.zeros((edge, LANES), f32)] * 5
+        for t in range(first, first + tiles // 2):
             if t < tiles - 1:
                 after = load(t + 1)
                 after_prim = primitives(after)
@@ -355,17 +368,49 @@
                 )
             before = flux
             cur, prim = after, after_prim
-        return carry
-
-    lax.fori_loop(0, boxes, box_step, 0)
-
-    src = iota((4 * LANES, LANES), 0)
-    col = iota((4 * LANES, LANES), 1)
-    shrink = jnp.where(
-        ((src // (2 * edge)) == col // half) & ((src & (edge - 1)) // 2 == (col & (half - 1))),
-        0.125,
-        0.0,
-    ).astype(jnp.bfloat16)
+        if not half_box:
+            for c in range(5):
+                carried[b, c] = before[c]
+
+    pairs = 5 * half
+    rx_copies = {}
+    for h in range(2):
+
+        def one_box(b, carry):
+            box_step(h, b)
+            start = b * 5 * edge
+            parts = [
+                nxt_state[t, pl.ds(start, pairs, stride=2), :]
+                + nxt_state[t, pl.ds(start + 1, pairs, stride=2), :]
+                for t in range(4 * h, 4 * h + 4)
+            ]
+            restr[b, h] = split_dot(jnp.concatenate(parts, axis=1), shrink, 2)
+            return carry
+
+        lax.fori_loop(0, boxes, one_box, 0)
+        for d in range(columns):
+            if d and not h:
+                reqx_copies[d].wait_recv()
+            if d:
+                rx_send[d, h] = restr[reqx_recv[d][0:1, :][0, 0], h]
+                rx_copies[d, h] = pltpu.make_async_remote_copy(
+                    rx_send.at[d, h], rx_recv.at[d, h], rx_ss.at[d * 3 + h], rx_rs.at[d * 3 + h],
+                    device_id=col_dev(lax.rem(gx + columns - d, columns)), device_id_type=MESH,
+                )
+                rx_copies[d, h].start()
+            else:
+                rx_recv[d, h] = restr[wanted[0:1, :][0, 0], h]
+
+    src = iota((2 * LANES, LANES), 0)
+    col = iota((2 * LANES, LANES), 1)
+    upper = src // LANES
+    src = src & (LANES - 1)
+    src_t = src & (SUBS - 1)
+    src_q = (src & (edge - 1)) // SUBS
+    to_z = ((src_t & 3) * 2 + src // (2 * edge)) * half + upper * SUBS + (src_t // 4) * 4 + src_q
+    to_y = upper * (LANES // 2) + src // 2
+    pool_z = jnp.where(col == to_z, 0.125, 0.0).astype(jnp.bfloat16)
+    pool_y = jnp.where(col == to_y, 0.125, 0.0).astype(jnp.bfloat16)
 
     for d in range(1, line):
         rep_copies[d].wait_recv()
@@ -385,13 +430,38 @@
                 flux = twice_flux(pair[0], pair[1])
                 scale = 0.5 * COURANT
             for c in range(5):
-                flux_d[b * 6 + g, c] = scale * flux[c]
+                flux_d[pl.ds(((b * 6 + g) * 5 + c) * SUBS, SUBS), :] = scale * flux[c]
+
+    for b in range(boxes):
+        at = b * 6 * 5 * SUBS
+        parts = [flux_d[pl.ds(at + e, 20, stride=4), :] for e in range(4)]
+        pooled[b, 0:20, :] = split_dot(jnp.concatenate(parts, axis=1), shrink, 2)
+        for g, pool in ((2, pool_y), (4, pool_z)):
+            parts = []
+            for f in (g, g + 1):
+                at = (b * 6 + f) * 5 * SUBS
+                parts.append(flux_d[pl.ds(at, 20, stride=2), :] + flux_d[pl.ds(at + 1, 20, stride=2), :])
+            pooled[b, 10 * g : 10 * g + 20, :] = split_dot(jnp.concatenate(parts, axis=1), pool, 2)
+        pooled[b, 60:64, :] = jnp.zeros((4, LANES), f32)
+    for d in range(columns):
+        if d:
+            pool_send[d] = pooled[reqx_recv[d][0:1, :][0, 0]]
+            rx_copies[d, 2] = pltpu.make_async_remote_copy(
+                pool_send.at[d], pool_recv.at[d], rx_ss.at[d * 3 + 2], rx_rs.at[d * 3 + 2],
+                device_id=col_dev(lax.rem(gx + columns - d, columns)), device_id_type=MESH,
+            )
+            rx_copies[d, 2].start()
+        else:
+            pool_recv[d] = pooled[wanted[0:1, :][0, 0]]
 
     def add_faces(bc, carry):
         b = lax.div(bc, 5)
         c = bc - b * 5
         row = pl.multiple_of(bc * edge, edge)
-        d = [flux_d[b * 6 + g, c] for g in range(6)]
+        d = [
+            flux_d[pl.ds(pl.multiple_of(((b * 6 + g) * 5 + c) * SUBS, SUBS), SUBS), :]
+            for g in range(6)
+        ]
         for q in range(quarters):
             for t in range(tiles):
                 s = q * SUBS + t
@@ -426,36 +496,46 @@
         )
         stores[-1].start()
 
-    for h in range(2):
-        parts = []
-        for t in range(4 * h, 4 * h + 4):
-            parts.append(
-                nxt_state[t, pl.ds(0, boxes * 5 * half, stride=2), :]
-                + nxt_state[t, pl.ds(1, boxes * 5 * half, stride=2), :]
-            )
-        mean = split_dot(jnp.concatenate(parts, axis=1), shrink, 2)
-        for b in range(boxes):
-            restr[b, :, tile_at(h)] = mean[b * 5 * half : (b + 1) * 5 * half, :]
-
-    rx_copies = {}
-    for d in list(range(1, columns)) + [0]:
+    wide20 = iota((20, LANES), 1)
+    low_z = (wide20 & (half - 1)) == 0
+    high_z = (wide20 & (half - 1)) == half - 1
+    low_y = wide20 < half
+    high_y = wide20 >= LANES - half
+    for d in range(columns):
         if d:
-            reqx_copies[d].wait_recv()
-            which = reqx_recv[d][0:1, :][0, 0]
-            rx_send[d] = restr[which]
-            rx_copies[d] = pltpu.make_async_remote_copy(
-                rx_send.at[d], rx_recv.at[d], rx_ss.at[d], rx_rs.at[d],
-                device_id=col_dev(lax.rem(gx + columns - d, columns)), device_id_type=MESH,
-            )
-            rx_copies[d].start()
-        else:
-            rx_recv[0] = restr[wanted[0:1, :][0, 0]]
-    for d in range(1, columns):
-        rx_copies[d].wait_recv()
+            for h in range(3):
+                rx_copies[d, h].wait_recv()
+        x, y, z = (pool_recv[d, pl.ds(20 * i, 20), :] for i in range(3))
+        for q in range(quarters):
+            for h in range(2):
+                s = h * 4 + q
+                add = jnp.where(
+                    low_z,
+                    pltpu.roll(z, (-s) % LANES, 1),
+                    jnp.where(high_z, pltpu.roll(z, (half - 1 - SUBS - s) % LANES, 1), 0.0),
+                )
+                if h:
+                    add = add + jnp.where(high_y, pltpu.roll(y, (LANES - half - 64 - half * q) % LANES, 1), 0.0)
+                else:
+                    add = add + jnp.where(low_y, pltpu.roll(y, (-half * q) % LANES, 1), 0.0)
+                for c in range(5):
+                    at = c * half + 4 * q
+                    rows4 = rx_recv[d, h, at : at + 4, :] + add[4 * c : 4 * c + 4, :]
+                    rx_recv[d, h, at : at + 4, :] = rows4
+        for c in range(5):
+            for h in range(2):
+                for f in range(2):
+                    at = c * half + f * (half - 1)
+                    source = (f * 5 + c) * 2 + h
+                    rx_recv[d, h, at : at + 1, :] = (
+                        rx_recv[d, h, at : at + 1, :] + x[source : source + 1, :]
+                    )
     for c in range(blocks):
         part = pl.ds(c * 5 * half, 5 * half)
         flag = covered[0:1, :][0, c]
-        coarse_next[part, :] = jnp.where(flag > 0, rx_recv[cover_col[0:1, :][0, c]], coarse[part, :])
+        taken = rx_recv[cover_col[0:1, :][0, c]]
+        for h in range(2):
+            coarse_next[part, tile_at(h)] = jnp.where(flag > 0, taken[h], coarse[part, tile_at(h)])
     store_coarse = pltpu.make_async_copy(coarse_next, coarse_out, out_sem.at[0])
     store_coarse.start()
 
@@ -484,10 +564,10 @@
     fine_next, coarse_next = pl.pallas_call(
         functools.partial(kernel, dims),
         out_shape=(
-            jax.ShapeDtypeStruct((fine_rows, plane), f32),
-            jax.ShapeDtypeStruct((coarse_rows, small), f32),
+            pltpu.VMEM((fine_rows, plane), f32),
+            pltpu.VMEM((coarse_rows, small), f32),
         ),
-        in_specs=[pl.BlockSpec(memory_space=pl.ANY)] * 5,
+        in_specs=[pl.BlockSpec(memory_space=pltpu.HBM)] * 5,
         out_specs=(pl.BlockSpec(memory_space=pl.ANY),) * 2,
         scratch_shapes=[
             vmem((fine_rows, plane), f32),
@@ -496,8 +576,8 @@
             vmem((faces + 6 * blocks,) + layer, f32),
             vmem((2, 2 * coarse_rows, LANES), f32),
             vmem((2, blocks * comps * SUBS, LANES), f32),
-            vmem((faces,) + layer, f32),
-            vmem((boxes, comps * half, small), f32),
+            vmem((faces * comps * SUBS, LANES), f32),
+            vmem((boxes, 2, comps * half, LANES), f32),
             vmem((coarse_rows, small), f32),
             vmem((boxes, 6), i32),
             vmem((boxes, 6), i32),
@@ -509,15 +589,19 @@
             vmem((columns, SUBS, LANES), i32),
             vmem((line, slots) + layer, f32),
             vmem((line * slots,) + layer, f32),
-            vmem((columns, comps * half, small), f32),
-            vmem((columns, comps * half, small), f32),
+            vmem((columns, 2, comps * half, LANES), f32),
+            vmem((columns, 2, comps * half, LANES), f32),
+            vmem((boxes, comps, edge, LANES), f32),
+            vmem((boxes, 64, LANES), f32),
+            vmem((columns, 64, LANES), f32),
+            vmem((columns, 64, LANES), f32),
             dma((5,)),
             dma((1 + plane // LANES,)),
         ]
         + [dma((line,)), dma((line,)), dma((columns,)), dma((columns,))]
-        + [dma((line,)), dma((line,)), dma((columns,)), dma((columns,))],
+        + [dma((line,)), dma((line,)), dma((3 * columns,)), dma((3 * columns,))],
         compiler_params=pltpu.CompilerParams(
-            collective_id=0, has_side_effects=True, vmem_limit_bytes=62 * 1024 * 1024
+            collective_id=0, has_side_effects=True, vmem_limit_bytes=60 * 1024 * 1024
         ),
     )(
         fine_state.reshape(fine_rows, plane),

time: 31.3 us -> 27.9 us (0.89)
  Pallas kernels: 27.2 us -> 25.4 us
  local copies, waits for them, and re-layouts: 3.3 us -> 1.78 us
    pallas_call x1, Pallas kernels: 27.2 us -> 25.4 us  [body(): pl.pallas_call(functools.partial(kernel, dims), out_shape=(pltpu.VMEM((fi...]
    unnamed x4 -> x2, local copies, waits for them, and re-layouts: 3.3 us -> 1.78 us
where the time goes in v3:
time: 27.9 us; the launch traced here: 27.8 us
  Pallas kernels  25.4 us (91%)
  local copies, waits for them, and re-layouts  1.78 us (6%)
  between operations  0.64 us (2%)
    pallas_call x1, Pallas kernels, body(): pl.pallas_call(functools.partial(kernel, dims), out_shape=(pltpu.VMEM((fi...  25.4 us
    unnamed x2, local copies, waits for them, and re-layouts  1.78 us

profile of v3, /device:TPU:0, one launch (start us, length us, event | category | flops | bytes accessed | tf_op | source)
XLA Modules:
  0.0 27.8 jit_solution(1541230099270529963)
XLA Ops:
  0.6 25.4 %shard_map.68 = (f32[320,1024]{1,0:T(8,128)S(1)}, f32[320,256]{1,0:T(8,128)S(1)}) custom-call(f32[320,1024]{1,0:T(8,128)} %bitcast.7, f32[320,256]{1,0:T(8,128)} %bitcast.8, s32[2,6]{1,0:T(2,128)} %neigh_hbm.1, s32[2,6]{1,0:T(2,128)} %csrc_hbm.1, s32[1,4]{1,0:T(1,128)} %bitcast.9), custom_call_target="tpu_custom_call" | custom-call | tf_op jit(solution)/shard_map/pallas_call | solution.py:564
  26.0 1.1 %copy.9 = f32[2,5,32,1024]{3,2,1,0:T(8,128)} copy(f32[2,5,32,1024]{3,2,1,0:T(8,128)S(1)} %bitcast.5) | data formatting | bytes 2621440
  27.1 0.7 %copy.10 = f32[4,5,16,256]{3,2,1,0:T(8,128)} copy(f32[4,5,16,256]{3,2,1,0:T(8,128)S(1)} %bitcast.6) | data formatting | bytes 655360

commit v4 on v3

--- a/solution.py
+++ b/solution.py
@@ -90,16 +90,25 @@
     def col_dev(x):
         return (x, gy, gz)
 
-    load_fine = pltpu.make_async_copy(fine_hbm, fine, in_sem.at[0])
-    load_coarse = pltpu.make_async_copy(coarse_hbm, coarse, in_sem.at[1])
+    def tile_at(t):
+        return pl.ds(t * LANES, LANES)
+
+    load_fine = [
+        pltpu.make_async_copy(fine_hbm.at[:, tile_at(t)], fine.at[t], in_sem.at[5 + t])
+        for t in range(tiles)
+    ]
+    load_coarse = [
+        pltpu.make_async_copy(coarse_hbm.at[:, tile_at(t)], coarse.at[t], in_sem.at[t])
+        for t in range(2)
+    ]
     load_ids = [
         pltpu.make_async_copy(a, b, in_sem.at[2 + i])
         for i, (a, b) in enumerate(((neigh_hbm, neigh), (csrc_hbm, csrc), (cov_hbm, cov)))
     ]
     for load in load_ids:
         load.start()
-    load_fine.start()
-    load_coarse.start()
+    for load in load_fine + load_coarse:
+        load.start()
 
     barrier = pltpu.get_barrier_semaphore()
     for d in range(1, line):
@@ -172,140 +181,6 @@
     cover_col = jnp.where(covered, cover_col, 0)
     covered = jnp.where(covered, 1, 0)
 
-    pl.semaphore_wait(barrier, line - 1 + columns - 1)
-
-    req_copies = {}
-    for d in range(1, line):
-        req_copies[d] = pltpu.make_async_remote_copy(
-            req_send.at[d], req_recv.at[d], req_ss.at[d], req_rs.at[d],
-            device_id=line_dev(lax.rem(me + d, line)), device_id_type=MESH,
-        )
-        req_copies[d].start()
-    reqx_copies = {}
-    for d in range(1, columns):
-        reqx_copies[d] = pltpu.make_async_remote_copy(
-            reqx_send.at[d], reqx_recv.at[d], reqx_ss.at[d], reqx_rs.at[d],
-            device_id=col_dev(lax.rem(gx + d, columns)), device_id_type=MESH,
-        )
-        reqx_copies[d].start()
-
-    def tile_at(t):
-        return pl.ds(t * LANES, LANES)
-
-    in_edge = lane8 & (edge - 1)
-    group = lane8 // edge
-    load_fine.wait()
-
-    def fine_layers(bc, carry):
-        b = lax.div(bc, 5)
-        c = bc - b * 5
-        row = pl.multiple_of(bc * edge, edge)
-        z_low = jnp.zeros((SUBS, LANES), f32)
-        z_high = jnp.zeros((SUBS, LANES), f32)
-        y_low = jnp.zeros((SUBS, LANES), f32)
-        y_high = jnp.zeros((SUBS, LANES), f32)
-        for q in range(quarters):
-            for t in range(tiles):
-                block = fine[pl.ds(row + q * SUBS, SUBS), tile_at(t)]
-                s = q * SUBS + t
-                z_low = jnp.where(in_edge == s, pltpu.roll(block, s, 1), z_low)
-                z_high = jnp.where(in_edge == s, pltpu.roll(block, (s - edge + 1) % LANES, 1), z_high)
-                if t == 0:
-                    y_low = jnp.where(group == q, pltpu.roll(block, q * edge, 1), y_low)
-                if t == tiles - 1:
-                    y_high = jnp.where(
-                        group == q, pltpu.roll(block, (q * edge - (LANES - edge)) % LANES, 1), y_high
-                    )
-                if q == 0:
-                    table[b * 6, c, t : t + 1, :] = block[0:1, :]
-                if q == quarters - 1:
-                    table[b * 6 + 1, c, t : t + 1, :] = block[SUBS - 1 : SUBS, :]
-        table[b * 6 + 2, c] = y_low
-        table[b * 6 + 3, c] = y_high
-        table[b * 6 + 4, c] = z_low
-        table[b * 6 + 5, c] = z_high
-        return carry
-
-    lax.fori_loop(0, boxes * 5, fine_layers, 0)
-
-    load_coarse.wait()
-    small = half * half
-    src = iota((small, 2 * LANES), 0)
-    col = iota((small, 2 * LANES), 1)
-    lane_w = col & (LANES - 1)
-    y_src = (lane_w // edge) * ((half - 1) * half) + (lane_w & (edge - 1)) // 2
-    z_j = 4 * (lane_w & (SUBS - 1)) + lane_w // edge
-    z_src = (z_j // 2) * half + ((lane_w & (edge - 1)) // SUBS) * (half - 1)
-    y_ok = (col < LANES) & (lane_w < 2 * edge) & (src == y_src)
-    z_ok = (col >= LANES) & ((lane_w & (edge - 1)) < 2 * SUBS) & (src == z_src)
-    lateral_table = jnp.where(y_ok | z_ok, 1.0, 0.0).astype(jnp.bfloat16)
-    lateral = split_dot(coarse[...], lateral_table, 3)
-    rows = blocks * 5 * half
-    for part in range(2):
-        piece = lateral[:, part * LANES : (part + 1) * LANES]
-        widened[part, pl.ds(0, rows, stride=2), :] = piece
-        widened[part, pl.ds(1, rows, stride=2), :] = piece
-    z_group = in_edge // SUBS
-
-    def coarse_layers(bc, carry):
-        b = lax.div(bc, 5)
-        c = bc - b * 5
-        row = pl.multiple_of(bc * edge, edge)
-        for f in range(2):
-            y = jnp.zeros((SUBS, LANES), f32)
-            z = jnp.zeros((SUBS, LANES), f32)
-            for q in range(quarters):
-                block = widened[0, pl.ds(row + q * SUBS, SUBS), :]
-                y = jnp.where(group == q, pltpu.roll(block, (edge * (q - f)) % LANES, 1), y)
-                block = widened[1, pl.ds(row + q * SUBS, SUBS), :]
-                z = jnp.where(z_group == q, pltpu.roll(block, (SUBS * (q - f)) % LANES, 1), z)
-            x = jnp.zeros((SUBS, LANES), f32)
-            at = pl.multiple_of(bc * half, half)
-            for t in range(SUBS):
-                block = coarse[pl.ds(at + f * (half - SUBS), SUBS), tile_at(t // 4)]
-                line_row = block[f * (SUBS - 1) : f * (SUBS - 1) + 1, :]
-                line_row = jnp.broadcast_to(line_row, (SUBS, LANES))
-                x = jnp.where(sub8 == t, pltpu.roll(line_row, (-2 * half * (t % 4)) % LANES, 1), x)
-            rows_y[f, pl.ds(pl.multiple_of(bc * SUBS, SUBS), SUBS), :] = x
-            table[faces + b * 6 + 2 + f, c] = y
-            table[faces + b * 6 + 4 + f, c] = z
-        return carry
-
-    lax.fori_loop(0, blocks * 5, coarse_layers, 0)
-
-    src = iota((LANES, LANES), 0)
-    col = iota((LANES, LANES), 1)
-    x_table = jnp.where(
-        src == (col // (2 * edge)) * half + (col & (edge - 1)) // 2, 1.0, 0.0
-    ).astype(jnp.bfloat16)
-    for f in range(2):
-        spread = split_dot(rows_y[f], x_table, 3)
-        for b in range(blocks):
-            for c in range(5):
-                at = (b * 5 + c) * SUBS
-                table[faces + b * 6 + f, c] = spread[at : at + SUBS, :]
-
-    my_codes = asked[0:1, :]
-    rep_copies = {}
-    for d in list(range(1, line)) + [0]:
-        if d:
-            req_copies[d].wait_recv()
-            codes = req_recv[d][0:1, :]
-        else:
-            codes = my_codes
-        for k in range(slots):
-            layer = table[codes[0, k]]
-            if d:
-                rep_send[d, k] = layer
-            else:
-                replies[d * slots + k] = layer
-        if d:
-            rep_copies[d] = pltpu.make_async_remote_copy(
-                rep_send.at[d], replies.at[pl.ds(d * slots, slots)], rep_ss.at[d], rep_rs.at[d],
-                device_id=line_dev(lax.rem(me + line - d, line)), device_id_type=MESH,
-            )
-            rep_copies[d].start()
-
     src = iota((4 * LANES, LANES), 0)
     col = iota((4 * LANES, LANES), 1)
     shrink = jnp.where(
@@ -322,7 +197,7 @@
     def box_step(half_box, b):
         def load(t):
             return [
-                fine[pl.ds(pl.multiple_of((b * 5 + c) * edge, edge), edge), tile_at(t)]
+                fine[t, pl.ds(pl.multiple_of((b * 5 + c) * edge, edge), edge), :]
                 for c in range(5)
             ]
 
@@ -374,8 +249,8 @@
 
     pairs = 5 * half
     rx_copies = {}
-    for h in range(2):
-
+
+    def step_half(h):
         def one_box(b, carry):
             box_step(h, b)
             start = b * 5 * edge
@@ -388,6 +263,8 @@
             return carry
 
         lax.fori_loop(0, boxes, one_box, 0)
+
+    def send_half(h):
         for d in range(columns):
             if d and not h:
                 reqx_copies[d].wait_recv()
@@ -401,6 +278,144 @@
             else:
                 rx_recv[d, h] = restr[wanted[0:1, :][0, 0], h]
 
+    for load in load_fine:
+        load.wait()
+    step_half(0)
+
+    in_edge = lane8 & (edge - 1)
+    group = lane8 // edge
+    pl.semaphore_wait(barrier, line - 1 + columns - 1)
+
+    req_copies = {}
+    for d in range(1, line):
+        req_copies[d] = pltpu.make_async_remote_copy(
+            req_send.at[d], req_recv.at[d], req_ss.at[d], req_rs.at[d],
+            device_id=line_dev(lax.rem(me + d, line)), device_id_type=MESH,
+        )
+        req_copies[d].start()
+    reqx_copies = {}
+    for d in range(1, columns):
+        reqx_copies[d] = pltpu.make_async_remote_copy(
+            reqx_send.at[d], reqx_recv.at[d], reqx_ss.at[d], reqx_rs.at[d],
+            device_id=col_dev(lax.rem(gx + d, columns)), device_id_type=MESH,
+        )
+        reqx_copies[d].start()
+
+
+    def fine_layers(bc, carry):
+        b = lax.div(bc, 5)
+        c = bc - b * 5
+        row = pl.multiple_of(bc * edge, edge)
+        z_low = jnp.zeros((SUBS, LANES), f32)
+        z_high = jnp.zeros((SUBS, LANES), f32)
+        y_low = jnp.zeros((SUBS, LANES), f32)
+        y_high = jnp.zeros((SUBS, LANES), f32)
+        for q in range(quarters):
+            for t in range(tiles):
+                block = fine[t, pl.ds(row + q * SUBS, SUBS), :]
+                s = q * SUBS + t
+                z_low = jnp.where(in_edge == s, pltpu.roll(block, s, 1), z_low)
+                z_high = jnp.where(in_edge == s, pltpu.roll(block, (s - edge + 1) % LANES, 1), z_high)
+                if t == 0:
+                    y_low = jnp.where(group == q, pltpu.roll(block, q * edge, 1), y_low)
+                if t == tiles - 1:
+                    y_high = jnp.where(
+                        group == q, pltpu.roll(block, (q * edge - (LANES - edge)) % LANES, 1), y_high
+                    )
+        at = pl.ds(pl.multiple_of(c * SUBS, SUBS), SUBS)
+        for side, layer in enumerate((y_low, y_high, z_low, z_high)):
+            table[b * 6 + 2 + side, at, :] = layer
+        return carry
+
+    lax.fori_loop(0, boxes * 5, fine_layers, 0, unroll=2)
+    for b in range(boxes):
+        for f in range(2):
+            for t in range(tiles):
+                table[b * 6 + f, pl.ds(t, 5, stride=SUBS), :] = fine[
+                    t, pl.ds(b * 5 * edge + f * (edge - 1), 5, stride=edge), :
+                ]
+
+    send_half(0)
+
+    for load in load_coarse:
+        load.wait()
+    small = half * half
+    src = iota((small, 2 * LANES), 0)
+    col = iota((small, 2 * LANES), 1)
+    lane_w = col & (LANES - 1)
+    y_src = (lane_w // edge) * ((half - 1) * half) + (lane_w & (edge - 1)) // 2
+    z_j = 4 * (lane_w & (SUBS - 1)) + lane_w // edge
+    z_src = (z_j // 2) * half + ((lane_w & (edge - 1)) // SUBS) * (half - 1)
+    y_ok = (col < LANES) & (lane_w < 2 * edge) & (src == y_src)
+    z_ok = (col >= LANES) & ((lane_w & (edge - 1)) < 2 * SUBS) & (src == z_src)
+    lateral_table = jnp.where(y_ok | z_ok, 1.0, 0.0).astype(jnp.bfloat16)
+    lateral = split_dot(jnp.concatenate([coarse[0], coarse[1]], axis=1), lateral_table, 3)
+    rows = blocks * 5 * half
+    for part in range(2):
+        piece = lateral[:, part * LANES : (part + 1) * LANES]
+        widened[part, pl.ds(0, rows, stride=2), :] = piece
+        widened[part, pl.ds(1, rows, stride=2), :] = piece
+    z_group = in_edge // SUBS
+
+    def coarse_layers(bc, carry):
+        b = lax.div(bc, 5)
+        c = bc - b * 5
+        row = pl.multiple_of(bc * edge, edge)
+        for f in range(2):
+            y = jnp.zeros((SUBS, LANES), f32)
+            z = jnp.zeros((SUBS, LANES), f32)
+            for q in range(quarters):
+                block = widened[0, pl.ds(row + q * SUBS, SUBS), :]
+                y = jnp.where(group == q, pltpu.roll(block, (edge * (q - f)) % LANES, 1), y)
+                block = widened[1, pl.ds(row + q * SUBS, SUBS), :]
+                z = jnp.where(z_group == q, pltpu.roll(block, (SUBS * (q - f)) % LANES, 1), z)
+            at = pl.ds(pl.multiple_of(c * SUBS, SUBS), SUBS)
+            table[faces + b * 6 + 2 + f, at, :] = y
+            table[faces + b * 6 + 4 + f, at, :] = z
+        return carry
+
+    lax.fori_loop(0, blocks * 5, coarse_layers, 0, unroll=4)
+
+    src = iota((LANES, LANES), 0)
+    col = iota((LANES, LANES), 1)
+    x_table = jnp.where(
+        src == (col // (2 * edge)) * half + (col & (edge - 1)) // 2, 1.0, 0.0
+    ).astype(jnp.bfloat16)
+    for f in range(2):
+        for t in range(SUBS):
+            ends = coarse[t // 4, pl.ds(f * (half - 1), blocks * 5, stride=half), :]
+            rows_y[f, pl.ds(t, blocks * 5, stride=SUBS), :] = pltpu.roll(
+                ends, (-2 * half * (t % 4)) % LANES, 1
+            )
+        spread = split_dot(rows_y[f], x_table, 3)
+        for b in range(blocks):
+            at = b * 5 * SUBS
+            table[faces + b * 6 + f] = spread[at : at + 5 * SUBS, :]
+
+    my_codes = asked[0:1, :]
+    rep_copies = {}
+    for d in list(range(1, line)) + [0]:
+        if d:
+            req_copies[d].wait_recv()
+            codes = req_recv[d][0:1, :]
+        else:
+            codes = my_codes
+        for k in range(slots):
+            layer = table[codes[0, k]]
+            if d:
+                rep_send[d, k] = layer
+            else:
+                replies[d * slots + k] = layer
+        if d:
+            rep_copies[d] = pltpu.make_async_remote_copy(
+                rep_send.at[d], replies.at[pl.ds(d * slots, slots)], rep_ss.at[d], rep_rs.at[d],
+                device_id=line_dev(lax.rem(me + line - d, line)), device_id_type=MESH,
+            )
+            rep_copies[d].start()
+
+    step_half(1)
+    send_half(1)
+
     src = iota((2 * LANES, LANES), 0)
     col = iota((2 * LANES, LANES), 1)
     upper = src // LANES
@@ -421,7 +436,7 @@
             normal = g // 2 + 1
             pair = []
             for layers in (ghost_all, own_all):
-                u = [layers[c] for c in range(5)]
+                u = [layers[c * SUBS : (c + 1) * SUBS, :] for c in range(5)]
                 pair.append((u,) + physical(u, primitives(u), normal))
             if g % 2:
                 flux = twice_flux(pair[1], pair[0])
@@ -535,7 +550,7 @@
         flag = covered[0:1, :][0, c]
         taken = rx_recv[cover_col[0:1, :][0, c]]
         for h in range(2):
-            coarse_next[part, tile_at(h)] = jnp.where(flag > 0, taken[h], coarse[part, tile_at(h)])
+            coarse_next[part, tile_at(h)] = jnp.where(flag > 0, taken[h], coarse[h, part, :])
     store_coarse = pltpu.make_async_copy(coarse_next, coarse_out, out_sem.at[0])
     store_coarse.start()
 
@@ -545,6 +560,21 @@
     for store in stores:
         store.wait()
     store_coarse.wait()
+
+
+def write_kernel(fine, coarse, fine_out, coarse_out, sem):
+    rows = fine.shape[0] // 4
+    copies = [
+        pltpu.make_async_copy(
+            fine.at[pl.ds(i * rows, rows), :], fine_out.at[pl.ds(i * rows, rows), :], sem.at[i]
+        )
+        for i in range(4)
+    ]
+    copies.append(pltpu.make_async_copy(coarse, coarse_out, sem.at[4]))
+    for copy in copies:
+        copy.start()
+    for copy in copies:
+        copy.wait()
 
 
 def body(fine_state, coarse_state, neighbours, coarse_sources, covering):
@@ -560,7 +590,7 @@
     f32, i32 = jnp.float32, jnp.int32
     vmem = pltpu.VMEM
     dma = pltpu.SemaphoreType.DMA
-    layer = (comps, SUBS, LANES)
+    layer = (comps * SUBS, LANES)
     fine_next, coarse_next = pl.pallas_call(
         functools.partial(kernel, dims),
         out_shape=(
@@ -570,8 +600,8 @@
         in_specs=[pl.BlockSpec(memory_space=pltpu.HBM)] * 5,
         out_specs=(pl.BlockSpec(memory_space=pl.ANY),) * 2,
         scratch_shapes=[
-            vmem((fine_rows, plane), f32),
-            vmem((coarse_rows, small), f32),
+            vmem((plane // LANES, fine_rows, LANES), f32),
+            vmem((2, coarse_rows, LANES), f32),
             vmem((plane // LANES, fine_rows, LANES), f32),
             vmem((faces + 6 * blocks,) + layer, f32),
             vmem((2, 2 * coarse_rows, LANES), f32),
@@ -595,7 +625,7 @@
             vmem((boxes, 64, LANES), f32),
             vmem((columns, 64, LANES), f32),
             vmem((columns, 64, LANES), f32),
-            dma((5,)),
+            dma((5 + plane // LANES,)),
             dma((1 + plane // LANES,)),
         ]
         + [dma((line,)), dma((line,)), dma((columns,)), dma((columns,))]
@@ -610,6 +640,16 @@
         coarse_sources,
         covering.reshape(1, blocks),
     )
+    fine_next, coarse_next = pl.pallas_call(
+        write_kernel,
+        out_shape=(
+            pltpu.HBM((fine_rows, plane), f32),
+            pltpu.HBM((coarse_rows, small), f32),
+        ),
+        in_specs=[pl.BlockSpec(memory_space=pl.ANY)] * 2,
+        out_specs=(pl.BlockSpec(memory_space=pl.ANY),) * 2,
+        scratch_shapes=[dma((5,))],
+    )(fine_next, coarse_next)
     return fine_next.reshape(fine_state.shape), coarse_next.reshape(coarse_state.shape)
 
 

time: 27.9 us -> 76.7 us (2.75)
  Pallas kernels: 25.4 us -> 74.1 us
    pallas_call x0 -> x1, Pallas kernels: none -> 50.8 us  [body(): pl.pallas_call(write_kernel, out_shape=(pltpu.HBM((fine_rows, plane), f32...]
    pallas_call x1, Pallas kernels: 25.4 us -> 23.3 us  [body(): pl.pallas_call(functools.partial(kernel, dims), out_shape=(pltpu.VMEM((fi...]
    unnamed x2 -> x4, local copies, waits for them, and re-layouts: 1.78 us -> 1.78 us
where the time goes in v4:
time: 76.7 us; the launch traced here: 76.5 us
  Pallas kernels  74.1 us (97%)
  local copies, waits for them, and re-layouts  1.78 us (2%)
    pallas_call x1, Pallas kernels, body(): pl.pallas_call(write_kernel, out_shape=(pltpu.HBM((fine_rows, plane), f32...  50.8 us
    pallas_call x1, Pallas kernels, body(): pl.pallas_call(functools.partial(kernel, dims), out_shape=(pltpu.VMEM((fi...  23.3 us
    unnamed x4, local copies, waits for them, and re-layouts  1.78 us

profile of v4, /device:TPU:0, one launch (start us, length us, event | category | flops | bytes accessed | tf_op | source)
XLA Modules:
  0.0 76.5 jit_solution(11785657613033538597)
XLA Ops:
  0.6 23.3 %shard_map.68 = (f32[320,1024]{1,0:T(8,128)S(1)}, f32[320,256]{1,0:T(8,128)S(1)}) custom-call(f32[320,1024]{1,0:T(8,128)} %bitcast.5, f32[320,256]{1,0:T(8,128)} %bitcast.6, s32[2,6]{1,0:T(2,128)} %neigh_hbm.1, s32[2,6]{1,0:T(2,128)} %csrc_hbm.1, s32[1,4]{1,0:T(1,128)} %bitcast.7), custom_call_target="tpu_custom_call" | custom-call | tf_op jit(solution)/shard_map/pallas_call | solution.py:594
  24.0 0.0 copy-start
  24.0 1.0 %copy-done = f32[320,1024]{1,0:T(8,128)} copy-done((f32[320,1024]{1,0:T(8,128)}, f32[320,1024]{1,0:T(8,128)S(1)}, u32[]{:S(2)}) %copy-start) | copy-done | bytes 1310744
  25.0 0.0 copy-start.1
  25.0 0.7 copy-done.1
  25.8 50.8 %shard_map.69 = (f32[320,1024]{1,0:T(8,128)}, f32[320,256]{1,0:T(8,128)}) custom-call(f32[320,1024]{1,0:T(8,128)} %copy-done, f32[320,256]{1,0:T(8,128)} %copy-done.1), custom_call_target="tpu_custom_call" | custom-call | tf_op jit(solution)/shard_map/pallas_call | solution.py:643
Async XLA Ops:
  24.0 1.1 %copy-start = (f32[320,1024]{1,0:T(8,128)}, f32[320,1024]{1,0:T(8,128)S(1)}, u32[]{:S(2)}) copy-start(f32[320,1024]{1,0:T(8,128)S(1)} %get-tuple-element.6.fine) | copy-start | bytes 3932164
  25.0 0.7 copy-start.1

commit v5 on v4

--- a/solution.py
+++ b/solution.py
@@ -168,6 +168,10 @@
     for shift in (1, 2, 4):
         place_tile = place_tile + pltpu.roll(place_tile, shift, 0)
 
+    place_row = place_tile[0:1, :]
+    ghost_at = [place_row[0, i] for i in range(faces)]
+    own_codes = [asked[0:1, :][0, k] for k in range(slots)]
+
     cover = jnp.broadcast_to(ids[16:17, :], (SUBS, LANES))
     cover_dev = lax.div(cover, jnp.full_like(cover, boxes))
     cover_col = lax.div(cover_dev, jnp.full_like(cover, line)) - gx
@@ -180,6 +184,9 @@
         reqx_send[d] = jnp.broadcast_to(wanted[d : d + 1, :], (SUBS, LANES))
     cover_col = jnp.where(covered, cover_col, 0)
     covered = jnp.where(covered, 1, 0)
+    cover_at = [cover_col[0:1, :][0, c] for c in range(blocks)]
+    cover_flag = [covered[0:1, :][0, c] for c in range(blocks)]
+    sent_box = [wanted[0:1, :][0, 0]]
 
     src = iota((4 * LANES, LANES), 0)
     col = iota((4 * LANES, LANES), 1)
@@ -266,17 +273,15 @@
 
     def send_half(h):
         for d in range(columns):
-            if d and not h:
-                reqx_copies[d].wait_recv()
             if d:
-                rx_send[d, h] = restr[reqx_recv[d][0:1, :][0, 0], h]
+                rx_send[d, h] = restr[sent_box[d], h]
                 rx_copies[d, h] = pltpu.make_async_remote_copy(
                     rx_send.at[d, h], rx_recv.at[d, h], rx_ss.at[d * 3 + h], rx_rs.at[d * 3 + h],
                     device_id=col_dev(lax.rem(gx + columns - d, columns)), device_id_type=MESH,
                 )
                 rx_copies[d, h].start()
             else:
-                rx_recv[d, h] = restr[wanted[0:1, :][0, 0], h]
+                rx_recv[d, h] = restr[sent_box[0], h]
 
     for load in load_fine:
         load.wait()
@@ -335,6 +340,9 @@
                     t, pl.ds(b * 5 * edge + f * (edge - 1), 5, stride=edge), :
                 ]
 
+    for d in range(1, columns):
+        reqx_copies[d].wait_recv()
+    sent_box += [reqx_recv[d][0:1, :][0, 0] for d in range(1, columns)]
     send_half(0)
 
     for load in load_coarse:
@@ -392,16 +400,15 @@
             at = b * 5 * SUBS
             table[faces + b * 6 + f] = spread[at : at + 5 * SUBS, :]
 
-    my_codes = asked[0:1, :]
     rep_copies = {}
+    for d in range(1, line):
+        req_copies[d].wait_recv()
+    codes = [own_codes] + [
+        [req_recv[d][0:1, :][0, k] for k in range(slots)] for d in range(1, line)
+    ]
     for d in list(range(1, line)) + [0]:
-        if d:
-            req_copies[d].wait_recv()
-            codes = req_recv[d][0:1, :]
-        else:
-            codes = my_codes
         for k in range(slots):
-            layer = table[codes[0, k]]
+            layer = table[codes[d][k]]
             if d:
                 rep_send[d, k] = layer
             else:
@@ -431,7 +438,7 @@
         rep_copies[d].wait_recv()
     for b in range(boxes):
         for g in range(6):
-            ghost_all = replies[place_tile[0:1, :][0, b * 6 + g]]
+            ghost_all = replies[ghost_at[b * 6 + g]]
             own_all = table[b * 6 + g]
             normal = g // 2 + 1
             pair = []
@@ -460,14 +467,14 @@
         pooled[b, 60:64, :] = jnp.zeros((4, LANES), f32)
     for d in range(columns):
         if d:
-            pool_send[d] = pooled[reqx_recv[d][0:1, :][0, 0]]
+            pool_send[d] = pooled[sent_box[d]]
             rx_copies[d, 2] = pltpu.make_async_remote_copy(
                 pool_send.at[d], pool_recv.at[d], rx_ss.at[d * 3 + 2], rx_rs.at[d * 3 + 2],
                 device_id=col_dev(lax.rem(gx + columns - d, columns)), device_id_type=MESH,
             )
             rx_copies[d, 2].start()
         else:
-            pool_recv[d] = pooled[wanted[0:1, :][0, 0]]
+            pool_recv[d] = pooled[sent_box[0]]
 
     def add_faces(bc, carry):
         b = lax.div(bc, 5)
@@ -521,8 +528,9 @@
             for h in range(3):
                 rx_copies[d, h].wait_recv()
         x, y, z = (pool_recv[d, pl.ds(20 * i, 20), :] for i in range(3))
-        for q in range(quarters):
-            for h in range(2):
+        for h in range(2):
+            adds = []
+            for q in range(quarters):
                 s = h * 4 + q
                 add = jnp.where(
                     low_z,
@@ -530,27 +538,25 @@
                     jnp.where(high_z, pltpu.roll(z, (half - 1 - SUBS - s) % LANES, 1), 0.0),
                 )
                 if h:
-                    add = add + jnp.where(high_y, pltpu.roll(y, (LANES - half - 64 - half * q) % LANES, 1), 0.0)
+                    shift = (LANES - half - LANES // 2 - half * q) % LANES
+                    add = add + jnp.where(high_y, pltpu.roll(y, shift, 1), 0.0)
                 else:
                     add = add + jnp.where(low_y, pltpu.roll(y, (-half * q) % LANES, 1), 0.0)
-                for c in range(5):
-                    at = c * half + 4 * q
-                    rows4 = rx_recv[d, h, at : at + 4, :] + add[4 * c : 4 * c + 4, :]
-                    rx_recv[d, h, at : at + 4, :] = rows4
-        for c in range(5):
-            for h in range(2):
+                adds.append(add)
+            for c in range(5):
                 for f in range(2):
-                    at = c * half + f * (half - 1)
                     source = (f * 5 + c) * 2 + h
-                    rx_recv[d, h, at : at + 1, :] = (
-                        rx_recv[d, h, at : at + 1, :] + x[source : source + 1, :]
+                    add = jnp.concatenate(
+                        [part[4 * c : 4 * c + 4, :] for part in adds[2 * f : 2 * f + 2]], axis=0
                     )
+                    add = add + jnp.where(sub8 == f * (SUBS - 1), x[source : source + 1, :], 0.0)
+                    at = c * half + f * SUBS
+                    rx_recv[d, h, at : at + SUBS, :] = rx_recv[d, h, at : at + SUBS, :] + add
     for c in range(blocks):
         part = pl.ds(c * 5 * half, 5 * half)
-        flag = covered[0:1, :][0, c]
-        taken = rx_recv[cover_col[0:1, :][0, c]]
+        taken = rx_recv[cover_at[c]]
         for h in range(2):
-            coarse_next[part, tile_at(h)] = jnp.where(flag > 0, taken[h], coarse[h, part, :])
+            coarse_next[part, tile_at(h)] = jnp.where(cover_flag[c] > 0, taken[h], coarse[h, part, :])
     store_coarse = pltpu.make_async_copy(coarse_next, coarse_out, out_sem.at[0])
     store_coarse.start()
 
@@ -560,21 +566,6 @@
     for store in stores:
         store.wait()
     store_coarse.wait()
-
-
-def write_kernel(fine, coarse, fine_out, coarse_out, sem):
-    rows = fine.shape[0] // 4
-    copies = [
-        pltpu.make_async_copy(
-            fine.at[pl.ds(i * rows, rows), :], fine_out.at[pl.ds(i * rows, rows), :], sem.at[i]
-        )
-        for i in range(4)
-    ]
-    copies.append(pltpu.make_async_copy(coarse, coarse_out, sem.at[4]))
-    for copy in copies:
-        copy.start()
-    for copy in copies:
-        copy.wait()
 
 
 def body(fine_state, coarse_state, neighbours, coarse_sources, covering):
@@ -640,16 +631,6 @@
         coarse_sources,
         covering.reshape(1, blocks),
     )
-    fine_next, coarse_next = pl.pallas_call(
-        write_kernel,
-        out_shape=(
-            pltpu.HBM((fine_rows, plane), f32),
-            pltpu.HBM((coarse_rows, small), f32),
-        ),
-        in_specs=[pl.BlockSpec(memory_space=pl.ANY)] * 2,
-        out_specs=(pl.BlockSpec(memory_space=pl.ANY),) * 2,
-        scratch_shapes=[dma((5,))],
-    )(fine_next, coarse_next)
     return fine_next.reshape(fine_state.shape), coarse_next.reshape(coarse_state.shape)
 
 

time: 76.7 us -> 25.6 us (0.33)
  Pallas kernels: 74.1 us -> 23 us
    pallas_call x1 -> x0, Pallas kernels: 50.8 us -> none  [body(): pl.pallas_call(write_kernel, out_shape=(pltpu.HBM((fine_rows, plane), f32...]
    unnamed x4 -> x2, local copies, waits for them, and re-layouts: 1.78 us -> 1.78 us
where the time goes in v5:
time: 25.6 us; the launch traced here: 25.4 us
  Pallas kernels  23 us (90%)
  local copies, waits for them, and re-layouts  1.78 us (7%)
  between operations  0.64 us (2%)
    pallas_call x1, Pallas kernels, body(): pl.pallas_call(functools.partial(kernel, dims), out_shape=(pltpu.VMEM((fi...  23 us
    unnamed x2, local copies, waits for them, and re-layouts  1.78 us

profile of v5, /device:TPU:0, one launch (start us, length us, event | category | flops | bytes accessed | tf_op | source)
XLA Modules:
  0.0 25.4 jit_solution(10698784615313905210)
XLA Ops:
  0.6 23.0 %shard_map.68 = (f32[320,1024]{1,0:T(8,128)S(1)}, f32[320,256]{1,0:T(8,128)S(1)}) custom-call(f32[320,1024]{1,0:T(8,128)} %bitcast.7, f32[320,256]{1,0:T(8,128)} %bitcast.8, s32[2,6]{1,0:T(2,128)} %neigh_hbm.1, s32[2,6]{1,0:T(2,128)} %csrc_hbm.1, s32[1,4]{1,0:T(1,128)} %bitcast.9), custom_call_target="tpu_custom_call" | custom-call | tf_op jit(solution)/shard_map/pallas_call | solution.py:585
  23.6 1.1 %copy.9 = f32[2,5,32,1024]{3,2,1,0:T(8,128)} copy(f32[2,5,32,1024]{3,2,1,0:T(8,128)S(1)} %bitcast.5) | data formatting | bytes 2621440
  24.7 0.7 %copy.10 = f32[4,5,16,256]{3,2,1,0:T(8,128)} copy(f32[4,5,16,256]{3,2,1,0:T(8,128)S(1)} %bitcast.6) | data formatting | bytes 655360

commit v6 on v5

--- a/solution.py
+++ b/solution.py
@@ -67,7 +67,7 @@
     dims,
     fine_hbm, coarse_hbm, neigh_hbm, csrc_hbm, cov_hbm,
     fine_out, coarse_out,
-    fine, coarse, nxt_state, table, widened, rows_y, flux_d, restr, coarse_next,
+    fine, coarse, nxt_state, table, widened, rows_y, flux_d, restr,
     neigh, csrc, cov, ids, req_send, req_recv, reqx_send, reqx_recv, rep_send, replies, rx_send, rx_recv,
     carried, pooled, pool_send, pool_recv,
     in_sem, out_sem, req_ss, req_rs, reqx_ss, reqx_rs, rep_ss, rep_rs, rx_ss, rx_rs,
@@ -188,6 +188,25 @@
     cover_flag = [covered[0:1, :][0, c] for c in range(blocks)]
     sent_box = [wanted[0:1, :][0, 0]]
 
+    in_edge = lane8 & (edge - 1)
+    group = lane8 // edge
+    pl.semaphore_wait(barrier, line - 1 + columns - 1)
+
+    req_copies = {}
+    for d in range(1, line):
+        req_copies[d] = pltpu.make_async_remote_copy(
+            req_send.at[d], req_recv.at[d], req_ss.at[d], req_rs.at[d],
+            device_id=line_dev(lax.rem(me + d, line)), device_id_type=MESH,
+        )
+        req_copies[d].start()
+    reqx_copies = {}
+    for d in range(1, columns):
+        reqx_copies[d] = pltpu.make_async_remote_copy(
+            reqx_send.at[d], reqx_recv.at[d], reqx_ss.at[d], reqx_rs.at[d],
+            device_id=col_dev(lax.rem(gx + d, columns)), device_id_type=MESH,
+        )
+        reqx_copies[d].start()
+
     src = iota((4 * LANES, LANES), 0)
     col = iota((4 * LANES, LANES), 1)
     shrink = jnp.where(
@@ -287,24 +306,10 @@
         load.wait()
     step_half(0)
 
-    in_edge = lane8 & (edge - 1)
-    group = lane8 // edge
-    pl.semaphore_wait(barrier, line - 1 + columns - 1)
-
-    req_copies = {}
-    for d in range(1, line):
-        req_copies[d] = pltpu.make_async_remote_copy(
-            req_send.at[d], req_recv.at[d], req_ss.at[d], req_rs.at[d],
-            device_id=line_dev(lax.rem(me + d, line)), device_id_type=MESH,
-        )
-        req_copies[d].start()
-    reqx_copies = {}
     for d in range(1, columns):
-        reqx_copies[d] = pltpu.make_async_remote_copy(
-            reqx_send.at[d], reqx_recv.at[d], reqx_ss.at[d], reqx_rs.at[d],
-            device_id=col_dev(lax.rem(gx + d, columns)), device_id_type=MESH,
-        )
-        reqx_copies[d].start()
+        reqx_copies[d].wait_recv()
+    sent_box += [reqx_recv[d][0:1, :][0, 0] for d in range(1, columns)]
+    send_half(0)
 
 
     def fine_layers(bc, carry):
@@ -339,11 +344,6 @@
                 table[b * 6 + f, pl.ds(t, 5, stride=SUBS), :] = fine[
                     t, pl.ds(b * 5 * edge + f * (edge - 1), 5, stride=edge), :
                 ]
-
-    for d in range(1, columns):
-        reqx_copies[d].wait_recv()
-    sent_box += [reqx_recv[d][0:1, :][0, 0] for d in range(1, columns)]
-    send_half(0)
 
     for load in load_coarse:
         load.wait()
@@ -556,16 +556,12 @@
         part = pl.ds(c * 5 * half, 5 * half)
         taken = rx_recv[cover_at[c]]
         for h in range(2):
-            coarse_next[part, tile_at(h)] = jnp.where(cover_flag[c] > 0, taken[h], coarse[h, part, :])
-    store_coarse = pltpu.make_async_copy(coarse_next, coarse_out, out_sem.at[0])
-    store_coarse.start()
-
+            coarse_out[part, tile_at(h)] = jnp.where(cover_flag[c] > 0, taken[h], coarse[h, part, :])
     for copies in (req_copies, reqx_copies, rep_copies, rx_copies):
         for d in copies:
             copies[d].wait_send()
     for store in stores:
         store.wait()
-    store_coarse.wait()
 
 
 def body(fine_state, coarse_state, neighbours, coarse_sources, covering):
@@ -589,7 +585,7 @@
             pltpu.VMEM((coarse_rows, small), f32),
         ),
         in_specs=[pl.BlockSpec(memory_space=pltpu.HBM)] * 5,
-        out_specs=(pl.BlockSpec(memory_space=pl.ANY),) * 2,
+        out_specs=(pl.BlockSpec(memory_space=pl.ANY), pl.BlockSpec(memory_space=pltpu.VMEM)),
         scratch_shapes=[
             vmem((plane // LANES, fine_rows, LANES), f32),
             vmem((2, coarse_rows, LANES), f32),
@@ -599,7 +595,6 @@
             vmem((2, blocks * comps * SUBS, LANES), f32),
             vmem((faces * comps * SUBS, LANES), f32),
             vmem((boxes, 2, comps * half, LANES), f32),
-            vmem((coarse_rows, small), f32),
             vmem((boxes, 6), i32),
             vmem((boxes, 6), i32),
             vmem((1, blocks), i32),

time: 25.6 us -> 25.8 us (level)
  no operation moved by 1% of the time
where the time goes in v6:
time: 25.8 us; the launch traced here: 25.6 us
  Pallas kernels  23.2 us (90%)
  local copies, waits for them, and re-layouts  1.78 us (7%)
  between operations  0.64 us (2%)
    pallas_call x1, Pallas kernels, body(): pl.pallas_call(functools.partial(kernel, dims), out_shape=(pltpu.VMEM((fi...  23.2 us
    unnamed x2, local copies, waits for them, and re-layouts  1.78 us

profile of v6, /device:TPU:0, one launch (start us, length us, event | category | flops | bytes accessed | tf_op | source)
XLA Modules:
  0.0 25.6 jit_solution(12297305237937624370)
XLA Ops:
  0.6 23.2 %shard_map.68 = (f32[320,1024]{1,0:T(8,128)S(1)}, f32[320,256]{1,0:T(8,128)S(1)}) custom-call(f32[320,1024]{1,0:T(8,128)} %bitcast.7, f32[320,256]{1,0:T(8,128)} %bitcast.8, s32[2,6]{1,0:T(2,128)} %neigh_hbm.1, s32[2,6]{1,0:T(2,128)} %csrc_hbm.1, s32[1,4]{1,0:T(1,128)} %bitcast.9), custom_call_target="tpu_custom_call" | custom-call | tf_op jit(solution)/shard_map/pallas_call | solution.py:581
  23.9 1.1 %copy.9 = f32[2,5,32,1024]{3,2,1,0:T(8,128)} copy(f32[2,5,32,1024]{3,2,1,0:T(8,128)S(1)} %bitcast.5) | data formatting | bytes 2621440
  24.9 0.7 %copy.10 = f32[4,5,16,256]{3,2,1,0:T(8,128)} copy(f32[4,5,16,256]{3,2,1,0:T(8,128)S(1)} %bitcast.6) | data formatting | bytes 655360

commit v7 on v6

--- a/solution.py
+++ b/solution.py
@@ -357,7 +357,7 @@
     y_ok = (col < LANES) & (lane_w < 2 * edge) & (src == y_src)
     z_ok = (col >= LANES) & ((lane_w & (edge - 1)) < 2 * SUBS) & (src == z_src)
     lateral_table = jnp.where(y_ok | z_ok, 1.0, 0.0).astype(jnp.bfloat16)
-    lateral = split_dot(jnp.concatenate([coarse[0], coarse[1]], axis=1), lateral_table, 3)
+    lateral = split_dot(jnp.concatenate([coarse[0], coarse[1]], axis=1), lateral_table, 2)
     rows = blocks * 5 * half
     for part in range(2):
         piece = lateral[:, part * LANES : (part + 1) * LANES]
@@ -395,7 +395,7 @@
             rows_y[f, pl.ds(t, blocks * 5, stride=SUBS), :] = pltpu.roll(
                 ends, (-2 * half * (t % 4)) % LANES, 1
             )
-        spread = split_dot(rows_y[f], x_table, 3)
+        spread = split_dot(rows_y[f], x_table, 2)
         for b in range(blocks):
             at = b * 5 * SUBS
             table[faces + b * 6 + f] = spread[at : at + 5 * SUBS, :]

time: 25.8 us -> 25.7 us (level)
  no operation moved by 1% of the time
where the time goes in v7:
time: 25.7 us; the launch traced here: 25.5 us
  Pallas kernels  23.1 us (90%)
  local copies, waits for them, and re-layouts  1.78 us (7%)
  between operations  0.64 us (2%)
    pallas_call x1, Pallas kernels, body(): pl.pallas_call(functools.partial(kernel, dims), out_shape=(pltpu.VMEM((fi...  23.1 us
    unnamed x2, local copies, waits for them, and re-layouts  1.78 us

profile of v7, /device:TPU:0, one launch (start us, length us, event | category | flops | bytes accessed | tf_op | source)
XLA Modules:
  0.0 25.5 jit_solution(16842267060910804154)
XLA Ops:
  0.6 23.1 %shard_map.68 = (f32[320,1024]{1,0:T(8,128)S(1)}, f32[320,256]{1,0:T(8,128)S(1)}) custom-call(f32[320,1024]{1,0:T(8,128)} %bitcast.7, f32[320,256]{1,0:T(8,128)} %bitcast.8, s32[2,6]{1,0:T(2,128)} %neigh_hbm.1, s32[2,6]{1,0:T(2,128)} %csrc_hbm.1, s32[1,4]{1,0:T(1,128)} %bitcast.9), custom_call_target="tpu_custom_call" | custom-call | tf_op jit(solution)/shard_map/pallas_call | solution.py:581
  23.8 1.1 %copy.9 = f32[2,5,32,1024]{3,2,1,0:T(8,128)} copy(f32[2,5,32,1024]{3,2,1,0:T(8,128)S(1)} %bitcast.5) | data formatting | bytes 2621440
  24.8 0.7 %copy.10 = f32[4,5,16,256]{3,2,1,0:T(8,128)} copy(f32[4,5,16,256]{3,2,1,0:T(8,128)S(1)} %bitcast.6) | data formatting | bytes 655360
